TPU v7x, 32 devices: a whole 2x2x4 slice. The times are simulated.
32 devices in a mesh: dp: 8 (over y, x, core), seq: 4 (over z).
Axes of the slice: x: 2, y: 2, z: 4, core: 2. Of those that a mesh axis runs over, the one named last changes fastest.
Arguments:
- hidden_in: bfloat16 [8192, 2048], P(('dp', 'seq')), may hold values from -6 to 6
- mix_values: bfloat16 [8192, 4096], P(('dp', 'seq')), may hold values from -6 to 6
- mix_gate: bfloat16 [8192, 4096], P(('dp', 'seq')), may hold values from -6 to 6
- state_proj: bfloat16 [8192, 2048], P(('dp', 'seq')), may hold values from -2 to 2
- step_raw: bfloat16 [8192, 64], P(('dp', 'seq')), may hold values from -4 to 4
- step_bias: float32 [64], replicated, may hold values from -1 to 0.5
- decay_rate: float32 [64], replicated, may hold values from 0.1 to 40
- skip_gain: float32 [64], replicated, may hold values from 0.5 to 1.5
- norm_gain: float32 [4096], replicated, may hold values from 0.5 to 1.5
- out_weight: bfloat16 [4096, 2048], P('seq'), may hold values from -0.09375 to 0.09375
- ffn_gain: float32 [2048], replicated, may hold values from 0.5 to 1.5
- expert_ids: int32 [8192, 8], P(('dp', 'seq')), may hold values from 0 to 31, all different within a row; in each aligned block of 256 rows (0 to 255, 256 to 511, ...) at most 72 rows name the same one
- route_weights: float32 [8192, 8], P(('dp', 'seq')), may hold values from 0.05 to 0.25
- gate_up: bfloat16 [32, 2048, 1536], P(('dp', 'seq')), may hold values from -0.125 to 0.125
- down_proj: bfloat16 [32, 768, 2048], P(('dp', 'seq')), may hold values from -0.21875 to 0.21875
- doc_lengths: int32 [8, 3], P('dp'), may hold values from 1 to 768, 1024 in all within a row
Outputs:
- block_out: bfloat16 [8192, 2048], P(('dp', 'seq'))
Inputs may be any that keep to these rules, and one draw needn't show every extreme that they name: `expert_ids`: in the rows of one device (aligned blocks of 256 tokens) no expert is chosen more than 72 times, a bound that some block reaches; a token's 8 experts differ. `doc_lengths`: each row sums to 1024; its largest length is exactly three quarters of 1024, rounded down.
All inputs are finite; a program needn't handle non-finite values.
Results may differ from a plain program's by a relative error of at most 0.019.
Values may be sent and summed in bfloat16 or wider, within the bound.
A program may use at most 256 MiB of HBM per device.

v0:
```python
import jax
import jax.numpy as jnp
from jax import lax
from jax.sharding import PartitionSpec as P

D = 2048
HEADS = 64
HEADDIM = 64
STATE = 128
GROUPS = 8
SPAN = 256
FF = 768
TOP = 8


precise = lax.Precision.HIGHEST
epsilon = 1e-05


def segment_of(lengths, positions):
    bounds = jnp.cumsum(lengths)
    return jnp.sum((positions[:, None] >= bounds[None, :]).astype(jnp.int32), axis=1)


def span_pass(carry, inputs):
    carry_state, segment_before = carry
    values, step_sizes, log_decay, segment, b_group, c_group = inputs
    length = values.shape[0]
    per_group = values.shape[1] // b_group.shape[1]
    cumulated = jnp.cumsum(log_decay, axis=0)
    row_ids = jnp.arange(length)
    allowed = (row_ids[:, None] >= row_ids[None, :]) & (segment[:, None] == segment[None, :])
    spread = jnp.transpose(cumulated[:, None, :] - cumulated[None, :, :], (2, 0, 1))
    decays = jnp.where(allowed[None], jnp.exp(jnp.minimum(spread, 0.0)), 0.0)
    scores = jnp.einsum("ign,jgn->gij", c_group, b_group, precision=precise)
    scores = jnp.repeat(scores, per_group, axis=0)
    weights = decays * scores * jnp.transpose(step_sizes)[:, None, :]
    inside = jnp.einsum("hij,jhp->ihp", weights, values, precision=precise)
    c_heads = jnp.repeat(c_group, per_group, axis=1)
    b_heads = jnp.repeat(b_group, per_group, axis=1)
    living = (segment == segment_before).astype(jnp.float32)
    reach = living[:, None] * jnp.exp(cumulated)
    carried = (
        jnp.einsum("hpn,ihn->ihp", carry_state, c_heads, precision=precise) * reach[:, :, None]
    )
    final_log = cumulated[-1]
    tail_weight = (
        jnp.where(
            (segment == segment[-1])[:, None],
            jnp.exp(jnp.minimum(final_log[None, :] - cumulated, 0.0)),
            0.0,
        )
        * step_sizes
    )
    fresh_state = jnp.einsum(
        "jhp,jhn->hpn", values * tail_weight[:, :, None], b_heads, precision=precise
    )
    keep_factor = (segment[-1] == segment_before).astype(jnp.float32) * jnp.exp(final_log)
    carry_state = keep_factor[:, None, None] * carry_state + fresh_state
    return ((carry_state, segment[-1]), inside + carried)


def run_spans(values, step_sizes, log_decay, segment, b_group, c_group, zero_state, segment_before):
    number = values.shape[0] // SPAN

    def blocked(array):
        return array.reshape((number, SPAN) + array.shape[1:])

    inputs = tuple(
        (blocked(array) for array in (values, step_sizes, log_decay, segment, b_group, c_group))
    )
    (end_state, ignored), outputs = lax.scan(span_pass, (zero_state, segment_before), inputs)
    return (outputs.reshape(values.shape), end_state)


def gated_norm(mixed_out, gate, gain, groups):
    gated = mixed_out * jax.nn.silu(gate.astype(jnp.float32))
    parts = gated.reshape(gated.shape[0], groups, -1)
    scale = lax.rsqrt(jnp.mean(parts * parts, axis=-1, keepdims=True) + epsilon)
    return ((parts * scale).reshape(gated.shape) * gain[None, :]).astype(jnp.bfloat16)


def body(
    hidden_in,
    mix_values,
    mix_gate,
    state_proj,
    step_raw,
    step_bias,
    decay_rate,
    skip_gain,
    norm_gain,
    out_weight,
    ffn_gain,
    expert_ids,
    route_weights,
    gate_up,
    down_proj,
    doc_lengths,
):
    tok_dev = hidden_in.shape[0]
    seq_size = lax.axis_size("seq")
    dp_size = lax.axis_size("dp")
    seq_tok = tok_dev * seq_size
    seq_rank = lax.axis_index("seq")
    lengths = doc_lengths[0]
    values_in, gate_in, proj_in, steps_in = (
        lax.all_to_all(mix_values, "seq", split_axis=1, concat_axis=0, tiled=True),
        lax.all_to_all(mix_gate, "seq", split_axis=1, concat_axis=0, tiled=True),
        lax.all_to_all(state_proj, "seq", split_axis=1, concat_axis=0, tiled=True),
        lax.all_to_all(step_raw, "seq", split_axis=1, concat_axis=0, tiled=True),
    )
    local_heads = HEADS // seq_size
    local_groups = GROUPS // seq_size
    head_start = seq_rank * local_heads
    positions = jnp.arange(seq_tok, dtype=jnp.int32)
    segment = segment_of(lengths, positions)
    bias_here = lax.dynamic_slice_in_dim(step_bias, head_start, local_heads)
    rate_here = lax.dynamic_slice_in_dim(decay_rate, head_start, local_heads)
    skip_here = lax.dynamic_slice_in_dim(skip_gain, head_start, local_heads)
    gain_here = lax.dynamic_slice_in_dim(norm_gain, head_start * HEADDIM, local_heads * HEADDIM)
    step_sizes = jax.nn.softplus(steps_in.astype(jnp.float32) + bias_here[None, :])
    log_decay = -step_sizes * rate_here[None, :] / seq_tok
    values = values_in.astype(jnp.float32).reshape(seq_tok, local_heads, HEADDIM)
    projected = proj_in.astype(jnp.float32).reshape(seq_tok, local_groups, 2, STATE)
    zero_state = jnp.zeros((local_heads, HEADDIM, STATE), jnp.float32)
    mixed_out, ignored = run_spans(
        values,
        step_sizes,
        log_decay,
        segment,
        projected[:, :, 0],
        projected[:, :, 1],
        zero_state,
        jnp.array(-1, jnp.int32),
    )
    mixed_out = mixed_out + skip_here[None, :, None] * values
    normed_mix = gated_norm(
        mixed_out.reshape(seq_tok, local_heads * HEADDIM), gate_in, gain_here, local_groups
    )
    mixer_out = lax.psum_scatter(
        jnp.dot(normed_mix, out_weight, preferred_element_type=jnp.float32).astype(jnp.bfloat16),
        "seq",
        scatter_dimension=0,
        tiled=True,
    ).astype(jnp.float32)
    merged = lax.optimization_barrier(
        (hidden_in.astype(jnp.float32) + mixer_out).astype(jnp.bfloat16)
    )
    merged_f = merged.astype(jnp.float32)
    square_mean = jnp.mean(merged_f * merged_f, axis=-1, keepdims=True)
    normed = (merged_f * lax.rsqrt(square_mean + epsilon) * ffn_gain[None, :]).astype(jnp.bfloat16)
    exp_dev = gate_up.shape[0]
    experts = exp_dev * dp_size * seq_size
    capacity = max(2, (9 * tok_dev * TOP + 8 * experts - 1) // (8 * experts))
    flat_ids = expert_ids.reshape(-1)
    onehot = (flat_ids[:, None] == jnp.arange(experts, dtype=jnp.int32)[None, :]).astype(jnp.int32)
    ranks = jnp.sum((jnp.cumsum(onehot, axis=0) - onehot) * onehot, axis=1)
    slots = flat_ids * capacity + ranks
    outgoing = (
        jnp.zeros((experts * capacity, D), jnp.bfloat16)
        .at[slots]
        .set(jnp.repeat(normed, TOP, axis=0))
        .reshape(experts, capacity, D)
    )
    arrived = lax.all_to_all(outgoing, ("dp", "seq"), split_axis=0, concat_axis=0, tiled=True)
    shaped = arrived.reshape(-1, exp_dev, arrived.shape[1], D)
    hidden = jnp.einsum("secd,edf->secf", shaped, gate_up, preferred_element_type=jnp.float32)
    active = (jax.nn.silu(hidden[..., :FF]) * hidden[..., FF:]).astype(jnp.bfloat16)
    result = jnp.einsum(
        "secf,efd->secd", active, down_proj, preferred_element_type=jnp.float32
    ).astype(jnp.bfloat16)
    processed = result.reshape(arrived.shape)
    returned = lax.all_to_all(processed, ("dp", "seq"), split_axis=0, concat_axis=0, tiled=True)
    gathered = returned.reshape(experts * capacity, D)[slots].astype(jnp.float32)
    weighted = gathered * route_weights.reshape(-1)[:, None]
    moe_out = jnp.sum(weighted.reshape(tok_dev, TOP, D), axis=1)
    return (merged_f + moe_out).astype(jnp.bfloat16)


def solution(mesh):
    in_specs = (
        P(("dp", "seq"), None),
        P(("dp", "seq"), None),
        P(("dp", "seq"), None),
        P(("dp", "seq"), None),
        P(("dp", "seq"), None),
        P(),
        P(),
        P(),
        P(),
        P("seq", None),
        P(),
        P(("dp", "seq"), None),
        P(("dp", "seq"), None),
        P(("dp", "seq"), None, None),
        P(("dp", "seq"), None, None),
        P("dp", None),
    )
    out_specs = P(("dp", "seq"), None)
    return jax.shard_map(body, mesh=mesh, in_specs=in_specs, out_specs=out_specs, check_vma=False)
```

profile of v0, /device:TPU:0, one launch (start us, length us, event | category | flops | bytes accessed | tf_op | source)
XLA Modules:
  0.0 875.9 jit_solution(17251370290683836039)
XLA Ops:
  6.5 6.6 all-to-all-start
  18.8 4.2 all-to-all-start.2
  23.1 4.1 copy.92
  27.2 20.5 %all-to-all-done.2 = bf16[256,4,512]{2,0,1:T(8,128)(2,1)} async-done(((bf16[256,4,512]{2,0,1:T(8,128)(2,1)}), bf16[256,4,512]{2,0,1:T(8,128)(2,1)}, u32[]{:S(2)}, u32[]{:S(2)}) %all-to-all-start.2) | async-done | bytes 1048608 | tf_op jit(solution)/shard_map/all_to_all | solution.py:110
  47.7 4.5 all-to-all-start.1
  52.7 4.1 copy.101
  60.5 3.6 reshape.299
  64.1 5.3 fusion.43
  69.4 30.5 %all-to-all-done.1 = bf16[256,4,1024]{0,2,1:T(8,128)(2,1)} async-done(((bf16[256,4,1024]{0,2,1:T(8,128)(2,1)}), bf16[256,4,1024]{0,2,1:T(8,128)(2,1)}, u32[]{:S(2)}, u32[]{:S(2)}) %all-to-all-start.1) | async-done | bytes 2097184 | tf_op jit(solution)/shard_map/all_to_all | solution.py:108
  99.9 4.4 all-to-all-start.3
  104.7 5.5 convert_bitcast_fusion.2
  110.2 117.9 %while.15 = (s32[]{:T(128)}, f32[16,64,128]{2,1,0:T(8,128)}, s32[]{:T(128)}, f32[4,256,16,64]{1,3,2,0:T(8,128)}, s32[4,256]{1,0:T(4,128)S(1)}, /*index=5*/f32[4,...) while((s32[]{:T(128)}, f32[16,64,128]{2,1,0:T(8,128)}, ...), condition=%wide.region_5.6_spmd.clone, body=%wide.region_2.5_spmd.clone.sunk | while | flops 1819239168 | bytes 29255868 | solution.py:72
  115.1 3.5 fusion.68
  122.6 4.0 fusion.65
  126.6 7.7 fusion.69
  135.3 3.6 convolution_add_fusion.2
  144.3 3.5 fusion.68
  151.9 4.1 fusion.65
  156.0 7.6 fusion.69
  164.5 3.7 convolution_add_fusion.2
  173.7 3.5 fusion.68
  181.3 4.1 fusion.65
  185.4 7.6 fusion.69
  193.9 3.7 convolution_add_fusion.2
  203.1 3.5 fusion.68
  210.7 4.1 fusion.65
  214.7 7.6 fusion.69
  223.2 3.7 convolution_add_fusion.2
  228.1 6.9 copy.98
  235.0 6.0 multiply_reduce_fusion
  241.2 5.2 copy.122
  246.4 5.4 copy.99
  251.8 5.3 copy.100
  257.1 3.9 convert_bitcast_fusion.1
  261.1 5.4 copy.102
  266.5 5.3 copy.104
  271.8 5.7 fusion.25
  277.7 6.2 convolution_convert_fusion.1
  286.3 16.1 %reduce-window.26 = s32[32,16,128]{2,1,0:T(8,128)S(1)} reduce-window(s32[32,16,128]{2,1,0:T(8,128)} %fusion.37, s32[]{:T(128)} %constant.29.clone.1), window={size=1x1x128 pad=0_0x0_0x127_0}, to_apply=%region_9.10 | reduce-window | flops 8323072 | bytes 524292 | tf_op jit(solution)/shard_map/reduce-window.3
  308.4 53.9 %reduce-scatter.2.cloned.1.call-done = bf16[256,2048]{1,0:T(8,128)(2,1)} async-done(((bf16[1024,2048]{1,0:T(8,128)(2,1)}), bf16[256,2048]{1,0:T(8,128)(2,1)}) %reduce-scatter.2.cloned.1.call-update) | async-done | bytes 1048592 | tf_op jit(solution)/shard_map/reduce_scatter | solution.py:141
  366.5 18.0 %scatter_custom_fusion = bf16[2304,2048]{1,0:T(8,128)(2,1)} fusion(s32[2048]{0:T(1024)S(1)} %bitcast.248, bf16[]{:T(256)} %constant.73.clone.1, bf16[256,2048]{1,0:T(8,128)(2,1)} %fusion.32), kind=kCustom, calls=%fused_computation.45 | custom fusion | bytes 10485762 | tf_op jit(solution)/shard_map/scatter | solution.py:163
  384.5 210.2 %all_to_all.62 = bf16[32,72,2048]{2,1,0:T(8,128)(2,1)S(1)} all-to-all(bf16[32,72,2048]{2,1,0:T(8,128)(2,1)} %bitcast.229), channel_id=1, replica_groups=mesh['dp'=8,'seq'=4] {'dp','seq'}, dimensions={0} | all-to-all | bytes 18874368 | tf_op jit(solution)/shard_map/all_to_all | solution.py:166
  594.6 18.3 %convolution_bitcast_fusion.2 = f32[32,1,72,1536]{3,2,0,1:T(8,128)S(1)} fusion(bf16[32,72,2048]{2,1,0:T(8,128)(2,1)S(1)} %all_to_all.62, bf16[1,2048,1536]{2,1,0:T(8,128)(2,1)} %param.31), kind=kOutput, calls=%fused_computation.49 | convolution fusion | flops 14495514624 | bytes 29884416 | tf_op jit(solution)/shard_map/secd,edf->secf/dot_general | solution.py:168
  612.9 10.3 %convolution_convert_fusion = bf16[32,72,2048]{2,1,0:T(8,128)(2,1)} fusion(f32[32,1,72,1536]{3,2,0,1:T(8,128)S(1)} %convolution_bitcast_fusion.2, bf16[1,768,2048]{2,1,0:T(8,128)(2,1)S(1)} %copy-done), kind=kOutput, calls=%fused_computation.51 | convolution fusion | flops 7263092736 | bytes 26738688 | tf_op jit(solution)/shard_map/secf,efd->secd/dot_general | solution.py:170
  623.2 4.8 all-to-all-start.5
  628.2 203.7 %all-to-all-done.5 = bf16[32,72,2048]{2,1,0:T(8,128)(2,1)} async-done(((bf16[32,72,2048]{2,1,0:T(8,128)(2,1)}), bf16[32,72,2048]{2,1,0:T(8,128)(2,1)}, u32[]{:S(2)}, u32[]{:S(2)}) %all-to-all-start.5) | async-done | bytes 9437216 | tf_op jit(solution)/shard_map/all_to_all | solution.py:174
  831.9 21.2 %gather_fusion = bf16[2048,2048]{1,0:T(8,128)(2,1)} fusion(bf16[2304,2048]{1,0:T(8,128)(2,1)} %bitcast.35, s32[2048]{0:T(1024)S(1)} %broadcast_clamp_fusion), kind=kCustom, calls=%fused_computation | custom fusion | bytes 16785408 | tf_op jit(solution)/shard_map/gather | solution.py:175
  853.1 12.5 %fusion.18 = f32[256,2048]{1,0:T(8,128)} fusion(bf16[2048,2048]{1,0:T(8,128)(2,1)} %gather_fusion, f32[256,8]{1,0:T(8,128)S(1)} %copy.111), kind=kLoop, calls=%fused_computation.44 | loop fusion | flops 12058624 | bytes 10493952 | tf_op jit(solution)/shard_map/reduce_sum | solution.py:177
  (151 shorter events, 62.8 us)
Async XLA Ops:
  6.5 606.4 %copy-start = (bf16[1,768,2048]{2,1,0:T(8,128)(2,1)S(1)}, bf16[1,768,2048]{2,1,0:T(8,128)(2,1)}, u32[]{:S(2)}) copy-start(bf16[1,768,2048]{2,1,0:T(8,128)(2,1)} %param.32) | copy-start | bytes 9437188
  6.5 12.2 %all-to-all-start = ((bf16[256,4,16]{0,2,1:T(8,128)(2,1)}), bf16[256,4,16]{0,2,1:T(8,128)(2,1)S(1)}, u32[]{:S(2)}, u32[]{:S(2)}) async-start(bf16[256,4,16]{0,2,1:T(8,128)(2,1)} %bitcast.250), calls=%async_computation | async-start | bytes 65536 | tf_op jit(solution)/shard_map/all_to_all | solution.py:111
  18.8 28.9 %all-to-all-start.2 = ((bf16[256,4,512]{2,0,1:T(8,128)(2,1)}), bf16[256,4,512]{2,0,1:T(8,128)(2,1)}, u32[]{:S(2)}, u32[]{:S(2)}) async-start(bf16[256,4,512]{2,0,1:T(8,128)(2,1)} %bitcast.240), calls=%async_computation.2 | async-start | bytes 2097152 | tf_op jit(solution)/shard_map/all_to_all | solution.py:110
  23.0 29.1 %copy-start.7 = (f32[64]{0:T(128)S(1)}, f32[64]{0:T(128)}, u32[]{:S(2)}) copy-start(f32[64]{0:T(128)} %param.23) | copy-start | bytes 772
  23.0 29.2 %copy-start.8 = (f32[64]{0:T(128)S(1)}, f32[64]{0:T(128)}, u32[]{:S(2)}) copy-start(f32[64]{0:T(128)} %param.24) | copy-start | bytes 772
  23.0 29.3 %copy-start.9 = (s32[1,3]{1,0:T(1,128)S(1)}, s32[1,3]{1,0:T(1,128)}, u32[]{:S(2)}) copy-start(s32[1,3]{1,0:T(1,128)} %param.33) | copy-start | bytes 40
  23.1 29.6 %copy-start.10 = (f32[64]{0:T(128)S(1)}, f32[64]{0:T(128)}, u32[]{:S(2)}) copy-start(f32[64]{0:T(128)} %param.25) | copy-start | bytes 772
  47.7 52.2 %all-to-all-start.1 = ((bf16[256,4,1024]{0,2,1:T(8,128)(2,1)}), bf16[256,4,1024]{0,2,1:T(8,128)(2,1)}, u32[]{:S(2)}, u32[]{:S(2)}) async-start(bf16[256,4,1024]{0,2,1:T(8,128)(2,1)} %bitcast.237), calls=%async_computation.1 | async-start | bytes 4194304 | tf_op jit(solution)/shard_map/all_to_all | solution.py:108
  99.9 135.1 %all-to-all-start.3 = ((bf16[256,4,1024]{0,2,1:T(8,128)(2,1)}), bf16[256,4,1024]{0,2,1:T(8,128)(2,1)}, u32[]{:S(2)}, u32[]{:S(2)}) async-start(bf16[256,4,1024]{0,2,1:T(8,128)(2,1)} %bitcast.236), calls=%async_computation.3 | async-start | bytes 4194304 | tf_op jit(solution)/shard_map/all_to_all | solution.py:109
  104.3 258.0 %reduce-scatter.2.cloned.1.call-start = ((), (), s32[]{:S(2)}) async-start(), calls=%async_computation.7 | async-start | bytes 5242880 | tf_op jit(solution)/shard_map/reduce_scatter | solution.py:141
  111.3 0.7 copy-start.1
  140.5 0.7 copy-start.1
  169.9 0.7 copy-start.1
  199.3 0.7 copy-start.1
  266.5 5.4 dynamic-slice-start
  271.8 5.8 copy-start.6
  283.9 0.7 copy-start.3
  306.7 58.5 %copy-start.4 = (f32[2048]{0:T(1024)S(1)}, f32[2048]{0:T(1024)}, u32[]{:S(2)}) copy-start(f32[2048]{0:T(1024)} %param.28) | copy-start | bytes 24580
  364.3 1.0 copy-start.2
  623.2 4.8 copy-start.5
  623.2 208.7 %all-to-all-start.5 = ((bf16[32,72,2048]{2,1,0:T(8,128)(2,1)}), bf16[32,72,2048]{2,1,0:T(8,128)(2,1)}, u32[]{:S(2)}, u32[]{:S(2)}) async-start(bf16[32,72,2048]{2,1,0:T(8,128)(2,1)} %convolution_convert_fusion), calls=%async_computation.6 | async-start | bytes 18874368 | tf_op jit(solution)/shard_map/all_to_all | solution.py:174
Sparse Core Ops, SparseCore 0:
  284.1 78.2 reduce-scatter.1
where the time goes:
time: 887 us; the launch traced here: 876 us
  waiting for transfers between devices  312 us (35%)
  blocking collectives  210 us (24%)
  local copies, waits for them, and re-layouts  124 us (14%)
  matrix products  102 us (11%)
  other arithmetic  83.6 us (9%)
  starting transfers between devices  24.9 us (3%)
  between operations  13.9 us (2%)
    all_to_all x1, blocking collectives, body(): lax.all_to_all(outgoing, ('dp', 'seq'), split_axis=0, concat_axis=0, tile...  210 us
    all_to_all x1, waiting for transfers between devices, body(): lax.all_to_all(processed, ('dp', 'seq'), split_axis=0, concat_axis=0, til...  204 us
    reduce_scatter x1, waiting for transfers between devices, body(): lax.psum_scatter(jnp.dot(normed_mix, out_weight, preferred_element_type=j...  53.9 us
    dot_general x4, matrix products, span_pass(): inside = jnp.einsum('hij,jhp->ihp', weights, values, precision=precise)  30.6 us
    all_to_all x1, waiting for transfers between devices, body(): lax.all_to_all(mix_values, 'seq', split_axis=1, concat_axis=0, tiled=True)  30.5 us
    gather x1, local copies, waits for them, and re-layouts, body(): returned.reshape(experts * capacity, D)[slots].astype(jnp.float32)  21.2 us
    all_to_all x1, waiting for transfers between devices, body(): lax.all_to_all(state_proj, 'seq', split_axis=1, concat_axis=0, tiled=True)  20.5 us
    another operation x16, other arithmetic  19.3 us
  transfers between devices with their start and end apart: 6, of which 5 were waited for; matrix products, arithmetic and copies ran while one was open for 19% of the time, Pallas kernels for 0%

commit v1 on v0

v1 whole, which is shorter than its diff:
```python
import jax
import jax.numpy as jnp
from jax import lax
from jax.experimental import pallas as pl
from jax.experimental.pallas import tpu as pltpu
from jax.sharding import PartitionSpec as P

D = 2048
HEADS = 64
HEADDIM = 64
STATE = 128
GROUPS = 8
FF = 768
TOP = 8
PER = HEADS // GROUPS
WIDE = PER * HEADDIM
CHUNKS = 4

precise = lax.Precision.HIGHEST
epsilon = 1e-05
f32 = jnp.float32
bf16 = jnp.bfloat16


def mix_inside(x_ref, bc_ref, cols_ref, rows_ref, seg_col_ref, seg_row_ref, y_ref, state_ref):
    rows = x_ref.shape[0]
    b = bc_ref[:, :STATE]
    c = bc_ref[:, STATE:]
    scores = lax.dot_general(c, b, (((1,), (1,)), ((), ())), preferred_element_type=f32)
    i = lax.broadcasted_iota(jnp.int32, (rows, rows), 0)
    j = lax.broadcasted_iota(jnp.int32, (rows, rows), 1)
    allowed = (i >= j) & (seg_col_ref[...] == seg_row_ref[...])
    scores = jnp.where(allowed, scores, 0.0)
    low = lax.broadcasted_iota(jnp.int32, (rows, 2 * HEADDIM), 1) < HEADDIM
    cols = cols_ref[0]
    cum_rows = rows_ref[0]
    for pair in range(PER // 2):
        here = pl.ds(pair * 2 * HEADDIM, 2 * HEADDIM)
        h0, h1 = 2 * pair, 2 * pair + 1
        x = x_ref[:, here].astype(f32)
        step = jnp.where(low, cols[:, PER + h0 : PER + h0 + 1], cols[:, PER + h1 : PER + h1 + 1])
        tail = jnp.where(low, cols[:, 2 * PER + h0 : 2 * PER + h0 + 1], cols[:, 2 * PER + h1 : 2 * PER + h1 + 1])
        stepped = (x * step).astype(bf16)
        parts = []
        for h in (h0, h1):
            spread = cols[:, h : h + 1] - cum_rows[h : h + 1, :]
            weights = (jnp.exp(jnp.minimum(spread, 0.0)) * scores).astype(bf16)
            parts.append(jnp.dot(weights, stepped, preferred_element_type=f32))
        y_ref[:, here] = jnp.where(low, parts[0], parts[1])
        state_ref[0, :, here] = lax.dot_general(
            b, (x * tail).astype(bf16), (((0,), (0,)), ((), ())), preferred_element_type=f32
        ).astype(state_ref.dtype)


def mix_finish(y_ref, x_ref, bc_ref, gate_ref, state_ref, reach_ref, skip_ref, gain_ref, out_ref):
    rows = x_ref.shape[0]
    c = bc_ref[:, STATE:]
    carried = jnp.dot(c, state_ref[0], preferred_element_type=f32)
    low = lax.broadcasted_iota(jnp.int32, (rows, 2 * HEADDIM), 1) < HEADDIM
    reach = reach_ref[0]
    total = jnp.zeros((rows, 1), f32)
    parts = []
    for pair in range(PER // 2):
        at = slice(pair * 2 * HEADDIM, (pair + 1) * 2 * HEADDIM)
        h0, h1 = 2 * pair, 2 * pair + 1
        factor = jnp.where(low, reach[:, h0 : h0 + 1], reach[:, h1 : h1 + 1])
        mixed = y_ref[:, at] + carried[:, at] * factor + skip_ref[:, at] * x_ref[:, at].astype(f32)
        u = mixed * jax.nn.silu(gate_ref[:, at].astype(f32))
        total = total + jnp.sum(u * u, axis=1, keepdims=True)
        parts.append(u)
    scale = lax.rsqrt(total / WIDE + epsilon)
    for pair in range(PER // 2):
        at = slice(pair * 2 * HEADDIM, (pair + 1) * 2 * HEADDIM)
        out_ref[:, at] = (parts[pair] * scale * gain_ref[:, at]).astype(bf16)


def mixer(mix_values, mix_gate, state_proj, step_raw, step_bias, decay_rate, skip_gain, norm_gain, lengths):
    rows = mix_values.shape[0]
    seq_size = lax.axis_size("seq")
    rank = lax.axis_index("seq")
    seq_tok = rows * seq_size
    start = rank * rows
    bounds = jnp.cumsum(lengths)
    positions = start + jnp.arange(rows, dtype=jnp.int32)
    segment = jnp.sum((positions[:, None] >= bounds[None, :]).astype(jnp.int32), axis=1)
    before = jnp.where(rank == 0, -1, jnp.sum((start - 1 >= bounds).astype(jnp.int32)))
    last = jnp.sum((start + rows - 1 >= bounds).astype(jnp.int32))
    steps = jax.nn.softplus(step_raw.astype(f32) + step_bias[None, :])
    log_decay = -steps * decay_rate[None, :] / seq_tok
    ids = jnp.arange(rows)
    lower = (ids[:, None] >= ids[None, :]).astype(f32)
    cum = jnp.dot(lower, log_decay, precision=precise)
    final = cum[-1:]
    tail = jnp.where((segment == last)[:, None], jnp.exp(jnp.minimum(final - cum, 0.0)), 0.0) * steps
    reach = (segment == before).astype(f32)[:, None] * jnp.exp(cum)
    keep = (last == before).astype(f32) * jnp.exp(final[0])
    cols = jnp.stack([cum, steps, tail], axis=1).reshape(rows, 3, GROUPS, PER)
    cols = jnp.transpose(cols, (2, 0, 1, 3)).reshape(GROUPS, rows, 3 * PER)
    cum_rows = jnp.transpose(cum).reshape(GROUPS, PER, rows)
    reach = jnp.transpose(reach.reshape(rows, GROUPS, PER), (1, 0, 2))
    wide = pl.BlockSpec((rows, WIDE), lambda g: (0, g))
    proj = pl.BlockSpec((rows, 2 * STATE), lambda g: (0, g))
    vector = pl.BlockSpec((1, WIDE), lambda g: (0, g))
    states = pl.BlockSpec((1, STATE, WIDE), lambda g: (g, 0, 0))
    inside, local = pl.pallas_call(
        mix_inside,
        grid=(GROUPS,),
        in_specs=[
            wide,
            proj,
            pl.BlockSpec((1, rows, 3 * PER), lambda g: (g, 0, 0)),
            pl.BlockSpec((1, PER, rows), lambda g: (g, 0, 0)),
            pl.BlockSpec((rows, 1), lambda g: (0, 0)),
            pl.BlockSpec((1, rows), lambda g: (0, 0)),
        ],
        out_specs=[wide, states],
        out_shape=[
            jax.ShapeDtypeStruct((rows, HEADS * HEADDIM), f32),
            jax.ShapeDtypeStruct((GROUPS, STATE, WIDE), bf16),
        ],
        compiler_params=pltpu.CompilerParams(vmem_limit_bytes=40 * 2**20),
        cost_estimate=pl.CostEstimate(flops=10**10, bytes_accessed=10**7, transcendentals=4 * 10**6),
    )(mix_values, state_proj, cols, cum_rows, segment[:, None], segment[None, :])
    keep_wide = jnp.repeat(keep, HEADDIM).reshape(GROUPS, 1, WIDE)
    width = GROUPS // CHUNKS
    carried = []
    for chunk in range(CHUNKS):
        at = slice(chunk * width, (chunk + 1) * width)
        own, factor = local[at], keep_wide[at]
        total = jnp.zeros(own.shape, bf16)
        for hop in range(seq_size - 1):
            sent = (own.astype(f32) + factor * total.astype(f32)).astype(bf16)
            total = total + lax.ppermute(sent, "seq", [(hop, hop + 1)])
        carried.append(total)
    state_in = jnp.concatenate(carried, axis=0)
    return pl.pallas_call(
        mix_finish,
        grid=(GROUPS,),
        in_specs=[wide, wide, proj, wide, states, pl.BlockSpec((1, rows, PER), lambda g: (g, 0, 0)), vector, vector],
        out_specs=wide,
        out_shape=jax.ShapeDtypeStruct((rows, HEADS * HEADDIM), bf16),
        compiler_params=pltpu.CompilerParams(vmem_limit_bytes=40 * 2**20),
        cost_estimate=pl.CostEstimate(flops=10**9, bytes_accessed=10**7, transcendentals=10**6),
    )(
        inside,
        mix_values,
        state_proj,
        mix_gate,
        state_in,
        reach,
        jnp.repeat(skip_gain, HEADDIM)[None, :],
        norm_gain[None, :],
    )


def experts_of(arrived, gate_up, down_proj):
    hidden = jnp.dot(arrived, gate_up, preferred_element_type=f32)
    active = (jax.nn.silu(hidden[:, :FF]) * hidden[:, FF:]).astype(bf16)
    return jnp.dot(active, down_proj, preferred_element_type=f32).astype(bf16)


def routed(normed, expert_ids, route_weights, gate_up, down_proj):
    rows = normed.shape[0]
    dp_size, seq_size = lax.axis_size("dp"), lax.axis_size("seq")
    rank = lax.axis_index("seq")
    experts = dp_size * seq_size
    capacity = max(2, (9 * rows * TOP + 8 * experts - 1) // (8 * experts))
    all_ids = lax.all_gather(expert_ids, "seq")
    all_weights = lax.all_gather(route_weights, "seq")
    here = jnp.arange(dp_size, dtype=jnp.int32) * seq_size + rank
    hit = all_ids[:, :, :, None] == here
    chosen = jnp.any(hit, axis=2)
    gains = jnp.sum(jnp.where(hit, all_weights[:, :, :, None], 0.0), axis=2)
    ids = jnp.arange(rows)
    earlier = (ids[:, None] > ids[None, :]).astype(bf16)
    place = jnp.einsum("ij,sjd->sid", earlier, chosen.astype(bf16), preferred_element_type=f32)
    place = jnp.where(chosen, place, -1.0)
    slots = jnp.arange(capacity, dtype=jnp.int32).astype(f32)
    current = normed
    arrivals, spreads = [], []
    for offset in range(seq_size):
        source = lax.rem(rank - offset + seq_size, seq_size)
        place_here = lax.dynamic_index_in_dim(place, source, 0, keepdims=False)
        gains_here = lax.dynamic_index_in_dim(gains, source, 0, keepdims=False)
        taken = jnp.transpose(place_here)[:, None, :] == slots[None, :, None]
        outgoing = jnp.dot(
            taken.astype(bf16).reshape(dp_size * capacity, rows), current, preferred_element_type=f32
        ).astype(bf16)
        spread = jnp.where(place_here[:, :, None] == slots, gains_here[:, :, None], 0.0)
        spreads.append(spread.astype(bf16).reshape(rows, dp_size * capacity))
        if offset < seq_size - 1:
            current = lax.ppermute(current, "seq", [(i, (i + 1) % seq_size) for i in range(seq_size)])
        arrivals.append(
            lax.all_to_all(outgoing.reshape(dp_size, capacity, D), "dp", split_axis=0, concat_axis=0, tiled=True)
        )
    total = None
    for offset in list(range(1, seq_size)) + [0]:
        result = experts_of(arrivals[offset].reshape(-1, D), gate_up[0], down_proj[0])
        returned = lax.all_to_all(
            result.reshape(dp_size, capacity, D), "dp", split_axis=0, concat_axis=0, tiled=True
        )
        part = jnp.dot(spreads[offset], returned.reshape(-1, D), preferred_element_type=f32)
        if offset:
            part = lax.ppermute(
                part.astype(bf16), "seq", [(i, (i - offset) % seq_size) for i in range(seq_size)]
            ).astype(f32)
        total = part if total is None else total + part
    return total


def body(
    hidden_in,
    mix_values,
    mix_gate,
    state_proj,
    step_raw,
    step_bias,
    decay_rate,
    skip_gain,
    norm_gain,
    out_weight,
    ffn_gain,
    expert_ids,
    route_weights,
    gate_up,
    down_proj,
    doc_lengths,
):
    dp_size = lax.axis_size("dp")
    share = out_weight.shape[0] // dp_size
    own = lax.dynamic_slice_in_dim(out_weight, lax.axis_index("dp") * share, share)
    weight = lax.all_gather(own, ("seq", "dp"), tiled=True)
    normed_mix = mixer(
        mix_values, mix_gate, state_proj, step_raw, step_bias, decay_rate, skip_gain, norm_gain, doc_lengths[0]
    )
    mixer_out = jnp.dot(normed_mix, weight, preferred_element_type=f32)
    merged = lax.optimization_barrier((hidden_in.astype(f32) + mixer_out).astype(bf16))
    merged_f = merged.astype(f32)
    square_mean = jnp.mean(merged_f * merged_f, axis=-1, keepdims=True)
    normed = (merged_f * lax.rsqrt(square_mean + epsilon) * ffn_gain[None, :]).astype(bf16)
    moe_out = routed(normed, expert_ids, route_weights, gate_up, down_proj)
    return (merged_f + moe_out).astype(bf16)


def solution(mesh):
    both = P(("dp", "seq"), None)
    deep = P(("dp", "seq"), None, None)
    in_specs = (both, both, both, both, both, P(), P(), P(), P(), P("seq", None), P(), both, both, deep, deep, P("dp", None))
    return jax.shard_map(body, mesh=mesh, in_specs=in_specs, out_specs=both, check_vma=False)
```

time: 887 us -> 549 us (0.62); the launches traced: 876 us -> 548 us
  blocking collectives: 210 us -> 81 us
  local copies, waits for them, and re-layouts: 124 us -> 16.2 us
  other arithmetic: 83.6 us -> 9.7 us
  waiting for transfers between devices: 312 us -> 272 us
  starting transfers between devices: 24.9 us -> 55 us
  matrix products: 102 us -> 79 us
  Pallas kernels: 0 us -> 19.5 us
    all_to_all x1 -> x0, blocking collectives: 210 us -> none  [body(): lax.all_to_all(outgoing, ('dp', 'seq'), split_axis=0, concat_axis=0, tile...]
    ppermute x0 -> x18, waiting for transfers between devices: none -> 192 us  [the longest x3 90.3 us: routed(): lax.ppermute(current, 'seq', [(i, (i + 1) % seq_size) for i in range(seq_...]
    all_to_all x5 -> x8, waiting for transfers between devices: 258 us -> 80 us  [the longest x4 41.4 us: routed(): lax.all_to_all(result.reshape(dp_size, capacity, D), 'dp', split_axis=0,...]
    all_gather x0 -> x2, blocking collectives: none -> 81 us  [the longest x1 67.9 us: routed(): all_ids = lax.all_gather(expert_ids, 'seq')]
    reduce_scatter x1 -> x0, waiting for transfers between devices: 53.9 us -> none  [body(): lax.psum_scatter(jnp.dot(normed_mix, out_weight, preferred_element_type=j...]
    convert_element_type x5 -> x0, local copies, waits for them, and re-layouts: 25.1 us -> none  [the longest x2 10.8 us: gated_norm(): gated = mixed_out * jax.nn.silu(gate.astype(jnp.float32))]
    dot_general x19, matrix products: 102 us -> 79 us  [the longest x4 26.6 us: experts_of(): hidden = jnp.dot(arrived, gate_up, preferred_element_type=f32)]
    convert_element_type x11 -> x5, other arithmetic: 26.2 us -> 4.67 us  [the longest x3 4.03 us: mixer(): sent = (own.astype(f32) + factor * total.astype(f32)).astype(bf16)]
  transfers between devices with their start and end apart: 6 -> 27, of which waited for: 5 -> 14; matrix products, arithmetic and copies ran while one was open for 19% -> 13% of each run, Pallas kernels for 0% -> 4%
where the time goes in v1:
time: 549 us; the launch traced here: 548 us
  waiting for transfers between devices  272 us (50%)
  blocking collectives  81 us (15%)
  matrix products  79 us (14%)
  starting transfers between devices  55 us (10%)
  Pallas kernels  19.5 us (4%)
  local copies, waits for them, and re-layouts  16.2 us (3%)
  between operations  15.3 us (3%)
  other arithmetic  9.7 us (2%)
    ppermute x3, waiting for transfers between devices, routed(): lax.ppermute(current, 'seq', [(i, (i + 1) % seq_size) for i in range(seq_...  90.3 us
    all_gather x1, blocking collectives, routed(): all_ids = lax.all_gather(expert_ids, 'seq')  67.9 us
    ppermute x3, waiting for transfers between devices, routed(): lax.ppermute(part.astype(bf16), 'seq', [(i, (i - offset) % seq_size) for...  65.4 us
    all_to_all x4, waiting for transfers between devices, routed(): lax.all_to_all(result.reshape(dp_size, capacity, D), 'dp', split_axis=0,...  41.4 us
    all_to_all x4, waiting for transfers between devices, routed(): lax.all_to_all(outgoing.reshape(dp_size, capacity, D), 'dp', split_axis=0...  38.6 us
    ppermute x12, waiting for transfers between devices, mixer(): total = total + lax.ppermute(sent, 'seq', [(hop, hop + 1)])  36.7 us
    dot_general x4, matrix products, experts_of(): hidden = jnp.dot(arrived, gate_up, preferred_element_type=f32)  26.6 us
    all_to_all x4, starting transfers between devices, routed(): lax.all_to_all(result.reshape(dp_size, capacity, D), 'dp', split_axis=0,...  17.9 us
  transfers between devices with their start and end apart: 27, of which 14 were waited for; matrix products, arithmetic and copies ran while one was open for 13% of the time, Pallas kernels for 4%

profile of v1, /device:TPU:0, one launch (start us, length us, event | category | flops | bytes accessed | tf_op | source)
XLA Modules:
  0.0 548.1 jit_solution(13401981219764536201)
XLA Ops:
  6.5 2.0 constant_dynamic-slice_fusion
  16.9 1.6 copy-done.5
  21.0 10.5 %shard_map.154 = (f32[256,4096]{1,0:T(8,128)S(1)}, bf16[8,128,512]{2,1,0:T(8,128)(2,1)S(1)}) custom-call(bf16[256,4096]{1,0:T(8,128)(2,1)S(1)} %copy-done.5, bf16[256,2048]{1,0:T(8,128)(2,1)S(1)} %copy-done.10, f32[8,256,24]{2,1,0:T(8,128)S(1)} %copy-done.9, f32[8,8,256]{2,1,0:T(8,128)S(1)} %bitcast.148, s32[256,1]{1,0:T(8,128)S(1)} %copy.34.seg_col_ref, ...), custom_call_target="tpu_custom_call" | custom-call | flops 10000000000 | bytes 10000000 | tf_op jit(solution)/shard_map/pallas_call | solution.py:105
  31.8 5.2 collective-permute-start
  40.9 4.2 collective-permute-done
  45.1 11.2 %collective-permute-done.3 = bf16[2,128,512]{2,1,0:T(8,128)(2,1)S(1)} collective-permute-done((bf16[2,128,512]{2,1,0:T(8,128)(2,1)S(1)}, bf16[2,128,512]{2,1,0:T(8,128)(2,1)S(1)}, u32[]{:S(2)}, u32[]{:S(2)}) %collective-permute-start.3) | collective-permute-done | bytes 262176 | tf_op jit(solution)/shard_map/ppermute | solution.py:133
  56.3 11.2 %collective-permute-done.6 = bf16[2,128,512]{2,1,0:T(8,128)(2,1)S(1)} collective-permute-done((bf16[2,128,512]{2,1,0:T(8,128)(2,1)S(1)}, bf16[2,128,512]{2,1,0:T(8,128)(2,1)S(1)}, u32[]{:S(2)}, u32[]{:S(2)}) %collective-permute-start.6) | collective-permute-done | bytes 262176 | tf_op jit(solution)/shard_map/ppermute | solution.py:133
  67.5 10.0 %collective-permute-done.9 = bf16[2,128,512]{2,1,0:T(8,128)(2,1)S(1)} collective-permute-done((bf16[2,128,512]{2,1,0:T(8,128)(2,1)S(1)}, bf16[2,128,512]{2,1,0:T(8,128)(2,1)S(1)}, u32[]{:S(2)}, u32[]{:S(2)}) %collective-permute-start.9) | collective-permute-done | bytes 262176 | tf_op jit(solution)/shard_map/ppermute | solution.py:133
  78.9 1.4 collective-permute-start.1
  86.0 67.9 %all-gather = s32[1024,8]{0,1:T(8,128)S(1)} all-gather(s32[256,8]{0,1:T(8,128)S(1)} %copy-done.22), channel_id=2, replica_groups=mesh['dp'=8,'seq'=4] {'seq'}, dimensions={0}, use_global_device_ids=true | all-gather | bytes 40960 | tf_op jit(solution)/shard_map/all_gather | solution.py:168
  154.1 2.5 fusion.51
  163.3 8.9 %shard_map.155 = bf16[256,4096]{1,0:T(8,128)(2,1)S(1)} custom-call(f32[256,4096]{1,0:T(8,128)S(1)} %copy-done.3, bf16[256,4096]{1,0:T(8,128)(2,1)S(1)} %copy-done.6, bf16[256,2048]{1,0:T(8,128)(2,1)S(1)} %copy-done.11, bf16[256,4096]{1,0:T(8,128)(2,1)S(1)} %copy-done.7, bf16[8,128,512]{2,1,0:T(8,128)(2,1)S(1)} %pad_maximum_fusion.state_ref, ...), custom_call_target="tpu_custom_call" | custom-call | flops 1000000000 | bytes 10000000 | tf_op jit(solution)/shard_map/pallas_call | solution.py:136
  173.6 11.1 %fusion.28 = bf16[256,2048]{1,0:T(8,128)(2,1)S(1)} fusion(bf16[256,4096]{1,0:T(8,128)(2,1)} %copy-done.8, bf16[4096,2048]{1,0:T(8,128)(2,1)} %all-gather.4.cloned.1.call-done, bf16[256,2048]{1,0:T(8,128)(2,1)} %param.16), kind=kOutput, calls=%fused_computation.32 | convolution fusion | flops 4296540160 | bytes 20971520 | tf_op jit(solution)/shard_map/dot_general | solution.py:236
  185.7 2.2 convolution_convert_fusion
  188.0 4.4 all-to-all-start.6
  192.6 35.5 %collective-permute-done.12 = bf16[256,2048]{1,0:T(8,128)(2,1)S(1)} collective-permute-done((bf16[256,2048]{1,0:T(8,128)(2,1)}, bf16[256,2048]{1,0:T(8,128)(2,1)S(1)}, u32[]{:S(2)}, u32[]{:S(2)}) %collective-permute-start.12) | collective-permute-done | bytes 1048608 | tf_op jit(solution)/shard_map/ppermute | solution.py:192
  229.1 3.1 convolution_convert_fusion.3
  232.2 4.4 all-to-all-start
  236.7 27.4 %collective-permute-done.14 = bf16[256,2048]{1,0:T(8,128)(2,1)S(1)} collective-permute-done((bf16[256,2048]{1,0:T(8,128)(2,1)}, bf16[256,2048]{1,0:T(8,128)(2,1)S(1)}, u32[]{:S(2)}, u32[]{:S(2)}) %collective-permute-start.14) | collective-permute-done | bytes 1048608 | tf_op jit(solution)/shard_map/ppermute | solution.py:192
  265.1 2.2 convolution_convert_fusion.2
  267.3 4.4 all-to-all-start.2
  271.7 6.7 %fusion.6 = f32[576,1536]{1,0:T(8,128)S(1)} fusion(bf16[576,2048]{1,0:T(8,128)(2,1)} %bitcast.26, bf16[1,2048,1536]{2,1,0:T(8,128)(2,1)} %param.29), kind=kOutput, calls=%fused_computation.6 | convolution fusion | flops 3623878656 | bytes 12189696 | tf_op jit(solution)/shard_map/dot_general | solution.py:157
  278.3 3.5 fusion.16
  281.9 19.3 %all-to-all-done.2 = bf16[8,72,2048]{2,1,0:T(8,128)(2,1)} async-done(((bf16[8,72,2048]{2,1,0:T(8,128)(2,1)}), bf16[8,72,2048]{2,1,0:T(8,128)(2,1)}, u32[]{:S(2)}, u32[]{:S(2)}) %all-to-all-start.2) | async-done | bytes 2359328 | tf_op jit(solution)/shard_map/all_to_all | solution.py:194
  301.1 4.4 all-to-all-start.1
  305.6 27.4 %collective-permute-done.16 = bf16[256,2048]{1,0:T(8,128)(2,1)S(1)} collective-permute-done((bf16[256,2048]{1,0:T(8,128)(2,1)}, bf16[256,2048]{1,0:T(8,128)(2,1)S(1)}, u32[]{:S(2)}, u32[]{:S(2)}) %collective-permute-start.16) | collective-permute-done | bytes 1048608 | tf_op jit(solution)/shard_map/ppermute | solution.py:192
  333.0 2.2 convolution_convert_fusion.1
  335.1 4.4 all-to-all-start.4
  339.5 6.7 %fusion.4 = f32[576,1536]{1,0:T(8,128)S(1)} fusion(bf16[576,2048]{1,0:T(8,128)(2,1)} %bitcast.36, bf16[1,2048,1536]{2,1,0:T(8,128)(2,1)} %param.29), kind=kOutput, calls=%fused_computation.4 | convolution fusion | flops 3623878656 | bytes 12189696 | tf_op jit(solution)/shard_map/dot_general | solution.py:157
  346.2 3.5 fusion.19
  349.6 19.3 %all-to-all-done.4 = bf16[8,72,2048]{2,1,0:T(8,128)(2,1)} async-done(((bf16[8,72,2048]{2,1,0:T(8,128)(2,1)}), bf16[8,72,2048]{2,1,0:T(8,128)(2,1)}, u32[]{:S(2)}, u32[]{:S(2)}) %all-to-all-start.4) | async-done | bytes 2359328 | tf_op jit(solution)/shard_map/all_to_all | solution.py:194
  369.0 4.6 all-to-all-start.3
  373.6 6.7 %fusion.2 = f32[576,1536]{1,0:T(8,128)S(1)} fusion(bf16[576,2048]{1,0:T(8,128)(2,1)} %bitcast.44, bf16[1,2048,1536]{2,1,0:T(8,128)(2,1)} %param.29), kind=kOutput, calls=%fused_computation.2 | convolution fusion | flops 3623878656 | bytes 12189696 | tf_op jit(solution)/shard_map/dot_general | solution.py:157
  380.3 3.5 fusion.22
  383.7 19.1 %all-to-all-done.3 = bf16[8,72,2048]{2,1,0:T(8,128)(2,1)} async-done(((bf16[8,72,2048]{2,1,0:T(8,128)(2,1)}), bf16[8,72,2048]{2,1,0:T(8,128)(2,1)}, u32[]{:S(2)}, u32[]{:S(2)}) %all-to-all-start.3) | async-done | bytes 2359328 | tf_op jit(solution)/shard_map/all_to_all | solution.py:199
  402.8 4.5 all-to-all-start.5
  407.4 13.1 %all-gather.1 = f32[1024,8]{0,1:T(8,128)S(1)} all-gather(f32[256,8]{0,1:T(8,128)S(1)} %copy-done.23), channel_id=3, replica_groups=mesh['dp'=8,'seq'=4] {'seq'}, dimensions={0}, use_global_device_ids=true | all-gather | bytes 40960 | tf_op jit(solution)/shard_map/all_gather | solution.py:169
  420.6 6.7 %fusion = f32[576,1536]{1,0:T(8,128)S(1)} fusion(bf16[576,2048]{1,0:T(8,128)(2,1)} %bitcast.52, bf16[1,2048,1536]{2,1,0:T(8,128)(2,1)} %param.29), kind=kOutput, calls=%fused_computation | convolution fusion | flops 3623878656 | bytes 12189696 | tf_op jit(solution)/shard_map/dot_general | solution.py:157
  427.3 3.4 fusion.25
  430.7 6.1 %all-to-all-done.5 = bf16[8,72,2048]{2,1,0:T(8,128)(2,1)} async-done(((bf16[8,72,2048]{2,1,0:T(8,128)(2,1)}), bf16[8,72,2048]{2,1,0:T(8,128)(2,1)}, u32[]{:S(2)}, u32[]{:S(2)}) %all-to-all-start.5) | async-done | bytes 2359328 | tf_op jit(solution)/shard_map/all_to_all | solution.py:199
  436.8 4.4 all-to-all-start.7
  441.2 3.8 fusion.29
  445.4 3.7 fusion.30
  449.1 3.7 fusion.31
  452.8 1.6 collective-permute-start.17
  454.4 16.2 %all-to-all-done.7 = bf16[8,72,2048]{2,1,0:T(8,128)(2,1)} async-done(((bf16[8,72,2048]{2,1,0:T(8,128)(2,1)}), bf16[8,72,2048]{2,1,0:T(8,128)(2,1)}, u32[]{:S(2)}, u32[]{:S(2)}) %all-to-all-start.7) | async-done | bytes 2359328 | tf_op jit(solution)/shard_map/all_to_all | solution.py:199
  471.6 64.5 %collective-permute-done.15 = bf16[256,2048]{1,0:T(8,128)(2,1)} collective-permute-done((bf16[256,2048]{1,0:T(8,128)(2,1)}, bf16[256,2048]{1,0:T(8,128)(2,1)}, u32[]{:S(2)}, u32[]{:S(2)}) %collective-permute-start.15) | collective-permute-done | bytes 1048608 | tf_op jit(solution)/shard_map/ppermute | solution.py:204
  536.1 5.2 fusion.35
  (129 shorter events, 33.5 us)
Async XLA Ops:
  6.5 271.8 %copy-start = (bf16[1,768,2048]{2,1,0:T(8,128)(2,1)S(1)}, bf16[1,768,2048]{2,1,0:T(8,128)(2,1)}, u32[]{:S(2)}) copy-start(bf16[1,768,2048]{2,1,0:T(8,128)(2,1)} %param.30) | copy-start | bytes 9437188
  6.5 167.0 %all-gather.4.cloned.1.call-start = ((), (), s32[]{:S(2)}) async-start(), calls=%async_computation.8 | async-start | bytes 17301504 | tf_op jit(solution)/shard_map/all_gather | solution.py:232
  16.9 1.6 copy-start.5
  19.7 1.3 copy-start.10
  31.5 47.4 %copy-start.1 = (bf16[8,128,512]{2,1,0:T(8,128)(2,1)}, bf16[8,128,512]{2,1,0:T(8,128)(2,1)S(1)}, u32[]{:S(2)}) copy-start(bf16[8,128,512]{2,1,0:T(8,128)(2,1)S(1)} %get-tuple-element.8) | copy-start | bytes 3145732
  31.6 47.4 %copy-start.2 = (f32[256,4096]{1,0:T(8,128)}, f32[256,4096]{1,0:T(8,128)S(1)}, u32[]{:S(2)}) copy-start(f32[256,4096]{1,0:T(8,128)S(1)} %get-tuple-element.7.y_ref) | copy-start | bytes 12582916
  31.8 54.0 %copy-start.24 = (f32[64]{0:T(128)S(1)}, f32[64]{0:T(128)}, u32[]{:S(2)}) copy-start(f32[64]{0:T(128)} %param.23) | copy-start | bytes 772
  31.8 54.2 %copy-start.22 = (s32[256,8]{0,1:T(8,128)S(1)}, s32[256,8]{0,1:T(8,128)}, u32[]{:S(2)}) copy-start(s32[256,8]{0,1:T(8,128)} %param.27) | copy-start | bytes 24580
  31.8 13.3 %collective-permute-start = (bf16[2,128,512]{2,1,0:T(8,128)(2,1)S(1)}, bf16[2,128,512]{2,1,0:T(8,128)(2,1)S(1)}, u32[]{:S(2)}, u32[]{:S(2)}) collective-permute-start(bf16[2,128,512]{2,1,0:T(8,128)(2,1)S(1)} %get-tuple-element.33), channel_id=1, source_target_pairs={{0,1},{4,5},{8,9},{12,13},{16,17},{20,21},{24,25},{28,29}} | collective-permute-start | bytes 786440 | tf_op jit(solution)/shard_map/ppermute | solution.py:133
  37.0 19.3 %collective-permute-start.3 = (bf16[2,128,512]{2,1,0:T(8,128)(2,1)S(1)}, bf16[2,128,512]{2,1,0:T(8,128)(2,1)S(1)}, u32[]{:S(2)}, u32[]{:S(2)}) collective-permute-start(bf16[2,128,512]{2,1,0:T(8,128)(2,1)S(1)} %get-tuple-element.36), channel_id=1, source_target_pairs={{0,1},{4,5},{8,9},{12,13},{16,17},{20,21},{24,25},{28,29}} | collective-permute-start | bytes 786440 | tf_op jit(solution)/shard_map/ppermute | solution.py:133
  38.3 29.3 %collective-permute-start.6 = (bf16[2,128,512]{2,1,0:T(8,128)(2,1)S(1)}, bf16[2,128,512]{2,1,0:T(8,128)(2,1)S(1)}, u32[]{:S(2)}, u32[]{:S(2)}) collective-permute-start(bf16[2,128,512]{2,1,0:T(8,128)(2,1)S(1)} %get-tuple-element.35), channel_id=1, source_target_pairs={{0,1},{4,5},{8,9},{12,13},{16,17},{20,21},{24,25},{28,29}} | collective-permute-start | bytes 786440 | tf_op jit(solution)/shard_map/ppermute | solution.py:133
  39.6 38.0 %collective-permute-start.9 = (bf16[2,128,512]{2,1,0:T(8,128)(2,1)S(1)}, bf16[2,128,512]{2,1,0:T(8,128)(2,1)S(1)}, u32[]{:S(2)}, u32[]{:S(2)}) collective-permute-start(bf16[2,128,512]{2,1,0:T(8,128)(2,1)S(1)} %get-tuple-element.34), channel_id=1, source_target_pairs={{0,1},{4,5},{8,9},{12,13},{16,17},{20,21},{24,25},{28,29}} | collective-permute-start | bytes 786440 | tf_op jit(solution)/shard_map/ppermute | solution.py:133
  56.3 22.6 %copy-start.15 = (bf16[2,128,512]{2,1,0:T(8,128)(2,1)}, bf16[2,128,512]{2,1,0:T(8,128)(2,1)S(1)}, u32[]{:S(2)}) copy-start(bf16[2,128,512]{2,1,0:T(8,128)(2,1)S(1)} %collective-permute-done.3) | copy-start | bytes 786436
  67.5 12.8 %copy-start.16 = (bf16[2,128,512]{2,1,0:T(8,128)(2,1)}, bf16[2,128,512]{2,1,0:T(8,128)(2,1)S(1)}, u32[]{:S(2)}) copy-start(bf16[2,128,512]{2,1,0:T(8,128)(2,1)S(1)} %collective-permute-done.6) | copy-start | bytes 786436
  77.6 2.7 copy-start.17
  78.9 75.1 %collective-permute-start.1 = (bf16[2,128,512]{2,1,0:T(8,128)(2,1)}, bf16[2,128,512]{2,1,0:T(8,128)(2,1)}, u32[]{:S(2)}, u32[]{:S(2)}) collective-permute-start(bf16[2,128,512]{2,1,0:T(8,128)(2,1)} %get-tuple-element.29), channel_id=1, source_target_pairs={{1,2},{5,6},{9,10},{13,14},{17,18},{21,22},{25,26},{29,30}} | collective-permute-start | bytes 786440 | tf_op jit(solution)/shard_map/ppermute | solution.py:133
  80.3 73.7 %collective-permute-start.10 = (bf16[2,128,512]{2,1,0:T(8,128)(2,1)}, bf16[2,128,512]{2,1,0:T(8,128)(2,1)}, u32[]{:S(2)}, u32[]{:S(2)}) collective-permute-start(bf16[2,128,512]{2,1,0:T(8,128)(2,1)} %get-tuple-element.32), channel_id=1, source_target_pairs={{1,2},{5,6},{9,10},{13,14},{17,18},{21,22},{25,26},{29,30}} | collective-permute-start | bytes 786440 | tf_op jit(solution)/shard_map/ppermute | solution.py:133
  81.7 72.4 %collective-permute-start.4 = (bf16[2,128,512]{2,1,0:T(8,128)(2,1)}, bf16[2,128,512]{2,1,0:T(8,128)(2,1)}, u32[]{:S(2)}, u32[]{:S(2)}) collective-permute-start(bf16[2,128,512]{2,1,0:T(8,128)(2,1)} %get-tuple-element.30), channel_id=1, source_target_pairs={{1,2},{5,6},{9,10},{13,14},{17,18},{21,22},{25,26},{29,30}} | collective-permute-start | bytes 786440 | tf_op jit(solution)/shard_map/ppermute | solution.py:133
  83.1 71.0 %collective-permute-start.7 = (bf16[2,128,512]{2,1,0:T(8,128)(2,1)}, bf16[2,128,512]{2,1,0:T(8,128)(2,1)}, u32[]{:S(2)}, u32[]{:S(2)}) collective-permute-start(bf16[2,128,512]{2,1,0:T(8,128)(2,1)} %get-tuple-element.31), channel_id=1, source_target_pairs={{1,2},{5,6},{9,10},{13,14},{17,18},{21,22},{25,26},{29,30}} | collective-permute-start | bytes 786440 | tf_op jit(solution)/shard_map/ppermute | solution.py:133
  154.1 7.1 %copy-start.6 = (bf16[256,4096]{1,0:T(8,128)(2,1)S(1)}, bf16[256,4096]{1,0:T(8,128)(2,1)}, u32[]{:S(2)}) copy-start(bf16[256,4096]{1,0:T(8,128)(2,1)} %x_ref.3) | copy-start | bytes 6291460
  154.1 7.1 %copy-start.7 = (bf16[256,4096]{1,0:T(8,128)(2,1)S(1)}, bf16[256,4096]{1,0:T(8,128)(2,1)}, u32[]{:S(2)}) copy-start(bf16[256,4096]{1,0:T(8,128)(2,1)} %gate_ref.1) | copy-start | bytes 6291460
  154.1 7.1 %copy-start.11 = (bf16[256,2048]{1,0:T(8,128)(2,1)S(1)}, bf16[256,2048]{1,0:T(8,128)(2,1)}, u32[]{:S(2)}) copy-start(bf16[256,2048]{1,0:T(8,128)(2,1)} %bc_ref.3) | copy-start | bytes 3145732
  156.6 4.1 collective-permute-start.2
  157.3 3.5 collective-permute-start.5
  158.0 2.9 collective-permute-start.8
  158.7 2.3 collective-permute-start.11
  159.6 1.7 copy-start.12
  160.7 1.2 copy-start.4
  160.8 2.5 copy-start.3
  172.2 1.4 copy-start.8
  173.5 11.4 %copy-start.21 = (f32[2048]{0:T(1024)S(1)}, f32[2048]{0:T(1024)}, u32[]{:S(2)}) copy-start(f32[2048]{0:T(1024)} %param.26) | copy-start | bytes 24580
  184.7 3.3 copy-start.13
  185.3 2.7 copy-start.14
  188.0 44.2 %all-to-all-start.6 = ((bf16[8,72,2048]{2,1,0:T(8,128)(2,1)}), bf16[8,72,2048]{2,1,0:T(8,128)(2,1)}, u32[]{:S(2)}, u32[]{:S(2)}) async-start(bf16[8,72,2048]{2,1,0:T(8,128)(2,1)} %bitcast.153), calls=%async_computation.6 | async-start | bytes 4718592 | tf_op jit(solution)/shard_map/all_to_all | solution.py:194
  192.4 35.7 %collective-permute-start.12 = (bf16[256,2048]{1,0:T(8,128)(2,1)}, bf16[256,2048]{1,0:T(8,128)(2,1)S(1)}, u32[]{:S(2)}, u32[]{:S(2)}) collective-permute-start(bf16[256,2048]{1,0:T(8,128)(2,1)} %copy-done.14), channel_id=1, source_target_pairs={{0,1},{1,2},{2,3},{3,0},{4,5},{5,6},{6,7},{7,4},{8,9},{9,10},{10,1... | collective-permute-start | bytes 3145736 | tf_op jit(solution)/shard_map/ppermute | solution.py:192
  232.2 35.0 %all-to-all-start = ((bf16[8,72,2048]{2,1,0:T(8,128)(2,1)}), bf16[8,72,2048]{2,1,0:T(8,128)(2,1)}, u32[]{:S(2)}, u32[]{:S(2)}) async-start(bf16[8,72,2048]{2,1,0:T(8,128)(2,1)} %bitcast.152), calls=%async_computation | async-start | bytes 4718592 | tf_op jit(solution)/shard_map/all_to_all | solution.py:194
  236.6 27.5 %collective-permute-start.14 = (bf16[256,2048]{1,0:T(8,128)(2,1)}, bf16[256,2048]{1,0:T(8,128)(2,1)S(1)}, u32[]{:S(2)}, u32[]{:S(2)}) collective-permute-start(bf16[256,2048]{1,0:T(8,128)(2,1)} %copy-done.19), channel_id=1, source_target_pairs={{0,1},{1,2},{2,3},{3,0},{4,5},{5,6},{6,7},{7,4},{8,9},{9,10},{10,1... | collective-permute-start | bytes 3145736 | tf_op jit(solution)/shard_map/ppermute | solution.py:192
  267.3 33.9 %all-to-all-start.2 = ((bf16[8,72,2048]{2,1,0:T(8,128)(2,1)}), bf16[8,72,2048]{2,1,0:T(8,128)(2,1)}, u32[]{:S(2)}, u32[]{:S(2)}) async-start(bf16[8,72,2048]{2,1,0:T(8,128)(2,1)} %bitcast.155), calls=%async_computation.2 | async-start | bytes 4718592 | tf_op jit(solution)/shard_map/all_to_all | solution.py:194
  301.1 34.0 %all-to-all-start.1 = ((bf16[8,72,2048]{2,1,0:T(8,128)(2,1)}), bf16[8,72,2048]{2,1,0:T(8,128)(2,1)}, u32[]{:S(2)}, u32[]{:S(2)}) async-start(bf16[8,72,2048]{2,1,0:T(8,128)(2,1)} %bitcast.158), calls=%async_computation.1 | async-start | bytes 4718592 | tf_op jit(solution)/shard_map/all_to_all | solution.py:199
  305.5 27.5 %collective-permute-start.16 = (bf16[256,2048]{1,0:T(8,128)(2,1)}, bf16[256,2048]{1,0:T(8,128)(2,1)S(1)}, u32[]{:S(2)}, u32[]{:S(2)}) collective-permute-start(bf16[256,2048]{1,0:T(8,128)(2,1)} %copy-done.18), channel_id=1, source_target_pairs={{0,1},{1,2},{2,3},{3,0},{4,5},{5,6},{6,7},{7,4},{8,9},{9,10},{10,1... | collective-permute-start | bytes 3145736 | tf_op jit(solution)/shard_map/ppermute | solution.py:192
  335.1 33.8 %all-to-all-start.4 = ((bf16[8,72,2048]{2,1,0:T(8,128)(2,1)}), bf16[8,72,2048]{2,1,0:T(8,128)(2,1)}, u32[]{:S(2)}, u32[]{:S(2)}) async-start(bf16[8,72,2048]{2,1,0:T(8,128)(2,1)} %bitcast.154), calls=%async_computation.4 | async-start | bytes 4718592 | tf_op jit(solution)/shard_map/all_to_all | solution.py:194
  369.0 33.9 %all-to-all-start.3 = ((bf16[8,72,2048]{2,1,0:T(8,128)(2,1)}), bf16[8,72,2048]{2,1,0:T(8,128)(2,1)}, u32[]{:S(2)}, u32[]{:S(2)}) async-start(bf16[8,72,2048]{2,1,0:T(8,128)(2,1)} %bitcast.159), calls=%async_computation.3 | async-start | bytes 4718592 | tf_op jit(solution)/shard_map/all_to_all | solution.py:199
  402.8 4.5 copy-start.23
  402.8 34.0 %all-to-all-start.5 = ((bf16[8,72,2048]{2,1,0:T(8,128)(2,1)}), bf16[8,72,2048]{2,1,0:T(8,128)(2,1)}, u32[]{:S(2)}, u32[]{:S(2)}) async-start(bf16[8,72,2048]{2,1,0:T(8,128)(2,1)} %bitcast.157), calls=%async_computation.5 | async-start | bytes 4718592 | tf_op jit(solution)/shard_map/all_to_all | solution.py:199
  436.8 33.8 %all-to-all-start.7 = ((bf16[8,72,2048]{2,1,0:T(8,128)(2,1)}), bf16[8,72,2048]{2,1,0:T(8,128)(2,1)}, u32[]{:S(2)}, u32[]{:S(2)}) async-start(bf16[8,72,2048]{2,1,0:T(8,128)(2,1)} %bitcast.156), calls=%async_computation.7 | async-start | bytes 4718592 | tf_op jit(solution)/shard_map/all_to_all | solution.py:199
  445.0 26.6 %collective-permute-start.13 = (bf16[256,2048]{1,0:T(8,128)(2,1)}, bf16[256,2048]{1,0:T(8,128)(2,1)}, u32[]{:S(2)}, u32[]{:S(2)}) collective-permute-start(bf16[256,2048]{1,0:T(8,128)(2,1)} %fusion.29), channel_id=1, source_target_pairs={{0,3},{1,0},{2,1},{3,2},{4,7},{5,4},{6,5},{7,6},{8,11},{9,8},{10,9... | collective-permute-start | bytes 3145736 | tf_op jit(solution)/shard_map/ppermute | solution.py:204
  449.1 87.0 %collective-permute-start.15 = (bf16[256,2048]{1,0:T(8,128)(2,1)}, bf16[256,2048]{1,0:T(8,128)(2,1)}, u32[]{:S(2)}, u32[]{:S(2)}) collective-permute-start(bf16[256,2048]{1,0:T(8,128)(2,1)} %fusion.30), channel_id=1, source_target_pairs={{0,2},{1,3},{2,0},{3,1},{4,6},{5,7},{6,4},{7,5},{8,10},{9,11},{10,... | collective-permute-start | bytes 3145736 | tf_op jit(solution)/shard_map/ppermute | solution.py:204
  452.8 83.2 %collective-permute-start.17 = (bf16[256,2048]{1,0:T(8,128)(2,1)}, bf16[256,2048]{1,0:T(8,128)(2,1)}, u32[]{:S(2)}, u32[]{:S(2)}) collective-permute-start(bf16[256,2048]{1,0:T(8,128)(2,1)} %fusion.31), channel_id=1, source_target_pairs={{0,1},{1,2},{2,3},{3,0},{4,5},{5,6},{6,7},{7,4},{8,9},{9,10},{10,1... | collective-permute-start | bytes 3145736 | tf_op jit(solution)/shard_map/ppermute | solution.py:204
  (4 other events, 4.3 us)
Sparse Core Ops, SparseCore 0:
  10.2 130.3 all-gather.3

commit v2 on v1

--- a/solution.py
+++ b/solution.py
@@ -165,8 +165,13 @@
     rank = lax.axis_index("seq")
     experts = dp_size * seq_size
     capacity = max(2, (9 * rows * TOP + 8 * experts - 1) // (8 * experts))
-    all_ids = lax.all_gather(expert_ids, "seq")
-    all_weights = lax.all_gather(route_weights, "seq")
+    ring = [(i, (i + 1) % seq_size) for i in range(seq_size)]
+    routes = [jnp.concatenate([expert_ids.T.astype(f32), route_weights.T], axis=0)]
+    for _ in range(seq_size - 1):
+        routes.append(lax.ppermute(routes[-1], "seq", ring))
+    routes = jnp.stack(routes)
+    all_ids = jnp.transpose(routes[:, :TOP], (0, 2, 1)).astype(jnp.int32)
+    all_weights = jnp.transpose(routes[:, TOP:], (0, 2, 1))
     here = jnp.arange(dp_size, dtype=jnp.int32) * seq_size + rank
     hit = all_ids[:, :, :, None] == here
     chosen = jnp.any(hit, axis=2)
@@ -179,9 +184,8 @@
     current = normed
     arrivals, spreads = [], []
     for offset in range(seq_size):
-        source = lax.rem(rank - offset + seq_size, seq_size)
-        place_here = lax.dynamic_index_in_dim(place, source, 0, keepdims=False)
-        gains_here = lax.dynamic_index_in_dim(gains, source, 0, keepdims=False)
+        place_here = place[offset]
+        gains_here = gains[offset]
         taken = jnp.transpose(place_here)[:, None, :] == slots[None, :, None]
         outgoing = jnp.dot(
             taken.astype(bf16).reshape(dp_size * capacity, rows), current, preferred_element_type=f32
@@ -189,21 +193,27 @@
         spread = jnp.where(place_here[:, :, None] == slots, gains_here[:, :, None], 0.0)
         spreads.append(spread.astype(bf16).reshape(rows, dp_size * capacity))
         if offset < seq_size - 1:
-            current = lax.ppermute(current, "seq", [(i, (i + 1) % seq_size) for i in range(seq_size)])
+            current = lax.ppermute(current, "seq", ring)
         arrivals.append(
             lax.all_to_all(outgoing.reshape(dp_size, capacity, D), "dp", split_axis=0, concat_axis=0, tiled=True)
         )
+    order = list(range(1, seq_size)) + [0]
+    parts = []
     total = None
-    for offset in list(range(1, seq_size)) + [0]:
-        result = experts_of(arrivals[offset].reshape(-1, D), gate_up[0], down_proj[0])
+    for turn, offset in enumerate(order):
+        arrived = arrivals[offset]
+        if turn >= 2:
+            arrived, parts[turn - 2] = lax.optimization_barrier((arrived, parts[turn - 2]))
+        result = experts_of(arrived.reshape(-1, D), gate_up[0], down_proj[0])
         returned = lax.all_to_all(
             result.reshape(dp_size, capacity, D), "dp", split_axis=0, concat_axis=0, tiled=True
         )
         part = jnp.dot(spreads[offset], returned.reshape(-1, D), preferred_element_type=f32)
+        parts.append(part.astype(bf16) if offset else part)
+    for turn, offset in enumerate(order):
+        part = parts[turn]
         if offset:
-            part = lax.ppermute(
-                part.astype(bf16), "seq", [(i, (i - offset) % seq_size) for i in range(seq_size)]
-            ).astype(f32)
+            part = lax.ppermute(part, "seq", [(i, (i - offset) % seq_size) for i in range(seq_size)]).astype(f32)
         total = part if total is None else total + part
     return total
 

time: 549 us -> 562 us (1.024)
  blocking collectives: 81 us -> 0 us
  waiting for transfers between devices: 272 us -> 320 us
  starting transfers between devices: 55 us -> 93.6 us
    all_gather x2 -> x0, blocking collectives: 81 us -> none  [the longest x1 67.9 us: routed(): all_ids = lax.all_gather(expert_ids, 'seq')]
    ppermute x6 -> x9, waiting for transfers between devices: 156 us -> 223 us  [the longest x3 100 us: routed(): current = lax.ppermute(current, 'seq', ring)]
    ppermute x6 -> x9, starting transfers between devices: 2.4 us -> 42.8 us  [the longest x3 35.2 us: routed(): current = lax.ppermute(current, 'seq', ring)]
    ppermute x12, waiting for transfers between devices: 36.7 us -> 0.03 us  [mixer(): total = total + lax.ppermute(sent, 'seq', [(hop, hop + 1)])]
    all_gather x1, waiting for transfers between devices: 0.01 us -> 26.9 us  [body(): weight = lax.all_gather(own, ('seq', 'dp'), tiled=True)]
    all_to_all x4, waiting for transfers between devices: 41.4 us -> 30.9 us  [routed(): lax.all_to_all(result.reshape(dp_size, capacity, D), 'dp', split_axis=0,...]
    unnamed x50 -> x52, local copies, waits for them, and re-layouts: 10 us -> 13 us
  transfers between devices with their start and end apart: 27 -> 30, of which waited for: 14 -> 12; matrix products, arithmetic and copies ran while one was open for 13% -> 14% of each run, Pallas kernels for 4% -> 3%
where the time goes in v2:
time: 562 us; the launch traced here: 561 us
  waiting for transfers between devices  320 us (57%)
  starting transfers between devices  93.6 us (17%)
  matrix products  79.1 us (14%)
  local copies, waits for them, and re-layouts  19.8 us (4%)
  Pallas kernels  19.5 us (3%)
  between operations  15.3 us (3%)
  other arithmetic  13.7 us (2%)
    ppermute x3, waiting for transfers between devices, routed(): current = lax.ppermute(current, 'seq', ring)  100 us
    ppermute x3, waiting for transfers between devices, routed(): lax.ppermute(part, 'seq', [(i, (i - offset) % seq_size) for i in range(se...  85.3 us
    all_to_all x4, waiting for transfers between devices, routed(): lax.all_to_all(outgoing.reshape(dp_size, capacity, D), 'dp', split_axis=0...  38.5 us
    ppermute x3, waiting for transfers between devices, routed(): routes.append(lax.ppermute(routes[-1], 'seq', ring))  38 us
    ppermute x3, starting transfers between devices, routed(): current = lax.ppermute(current, 'seq', ring)  35.2 us
    all_to_all x4, waiting for transfers between devices, routed(): lax.all_to_all(result.reshape(dp_size, capacity, D), 'dp', split_axis=0,...  30.9 us
    all_gather x1, waiting for transfers between devices, body(): weight = lax.all_gather(own, ('seq', 'dp'), tiled=True)  26.9 us
    dot_general x4, matrix products, experts_of(): hidden = jnp.dot(arrived, gate_up, preferred_element_type=f32)  26.6 us
  transfers between devices with their start and end apart: 30, of which 12 were waited for; matrix products, arithmetic and copies ran while one was open for 14% of the time, Pallas kernels for 3%

profile of v2, /device:TPU:0, one launch (start us, length us, event | category | flops | bytes accessed | tf_op | source)
XLA Modules:
  0.0 560.7 jit_solution(6113099385900606580)
XLA Ops:
  6.5 2.0 constant_dynamic-slice_fusion
  10.6 3.0 collective-permute-start.12
  26.1 10.5 %shard_map.154 = (f32[256,4096]{1,0:T(8,128)S(1)}, bf16[8,128,512]{2,1,0:T(8,128)(2,1)S(1)}) custom-call(bf16[256,4096]{1,0:T(8,128)(2,1)S(1)} %copy-done.6, bf16[256,2048]{1,0:T(8,128)(2,1)S(1)} %copy-done.11, f32[8,256,24]{2,1,0:T(8,128)S(1)} %copy-done.10, f32[8,8,256]{2,1,0:T(8,128)S(1)} %bitcast.158, s32[256,1]{1,0:T(8,128)S(1)} %copy.34.seg_col_ref, ...), custom_call_target="tpu_custom_call" | custom-call | flops 10000000000 | bytes 10000000 | tf_op jit(solution)/shard_map/pallas_call | solution.py:105
  36.7 2.0 copy-done.3
  40.7 3.5 collective-permute-start
  44.2 2.0 collective-permute-start.3
  46.2 2.0 collective-permute-start.6
  48.2 2.0 collective-permute-start.9
  50.7 37.0 %collective-permute-done.13 = f32[16,256]{1,0:T(8,128)S(1)} collective-permute-done((f32[16,256]{1,0:T(8,128)}, f32[16,256]{1,0:T(8,128)S(1)}, u32[]{:S(2)}, u32[]{:S(2)}) %collective-permute-start.13) | collective-permute-done | bytes 16416 | tf_op jit(solution)/shard_map/ppermute | solution.py:171
  87.8 2.5 collective-permute-start.14
  99.0 1.8 fusion.51
  107.5 8.9 %shard_map.155 = bf16[256,4096]{1,0:T(8,128)(2,1)S(1)} custom-call(f32[256,4096]{1,0:T(8,128)S(1)} %copy-done.4, bf16[256,4096]{1,0:T(8,128)(2,1)S(1)} %copy-done.7, bf16[256,2048]{1,0:T(8,128)(2,1)S(1)} %copy-done.12, bf16[256,4096]{1,0:T(8,128)(2,1)S(1)} %copy-done.8, bf16[8,128,512]{2,1,0:T(8,128)(2,1)S(1)} %pad_maximum_fusion.state_ref, ...), custom_call_target="tpu_custom_call" | custom-call | flops 1000000000 | bytes 10000000 | tf_op jit(solution)/shard_map/pallas_call | solution.py:136
  117.8 26.9 %all-gather.2.cloned.1.call-done = bf16[4096,2048]{1,0:T(8,128)(2,1)} async-done(((bf16[128,2048]{1,0:T(8,128)(2,1)}), bf16[4096,2048]{1,0:T(8,128)(2,1)}) %all-gather.2.cloned.1.call-update) | async-done | bytes 16777232 | tf_op jit(solution)/shard_map/all_gather | solution.py:242
  144.8 11.1 %fusion.28 = bf16[256,2048]{1,0:T(8,128)(2,1)S(1)} fusion(bf16[256,4096]{1,0:T(8,128)(2,1)} %copy-done.9, bf16[4096,2048]{1,0:T(8,128)(2,1)} %all-gather.2.cloned.1.call-done, bf16[256,2048]{1,0:T(8,128)(2,1)} %param.16), kind=kOutput, calls=%fused_computation.32 | convolution fusion | flops 4296540160 | bytes 20971520 | tf_op jit(solution)/shard_map/dot_general | solution.py:246
  157.0 2.2 convolution_convert_fusion.1
  159.2 4.6 all-to-all-start.3
  163.8 35.1 %collective-permute-start.15 = (bf16[256,2048]{1,0:T(8,128)(2,1)}, bf16[256,2048]{1,0:T(8,128)(2,1)S(1)}, u32[]{:S(2)}, u32[]{:S(2)}) collective-permute-start(bf16[256,2048]{1,0:T(8,128)(2,1)} %copy-done.15), channel_id=1, source_target_pairs={{0,1},{1,2},{2,3},{3,0},{4,5},{5,6},{6,7},{7,4},{8,9},{9,10},{10,1... | collective-permute-start | bytes 3145736 | tf_op jit(solution)/shard_map/ppermute | solution.py:196
  198.9 45.3 %collective-permute-done.15 = bf16[256,2048]{1,0:T(8,128)(2,1)S(1)} collective-permute-done((bf16[256,2048]{1,0:T(8,128)(2,1)}, bf16[256,2048]{1,0:T(8,128)(2,1)S(1)}, u32[]{:S(2)}, u32[]{:S(2)}) %collective-permute-start.15) | collective-permute-done | bytes 1048608 | tf_op jit(solution)/shard_map/ppermute | solution.py:196
  245.2 3.2 convolution_convert_fusion.2
  248.3 4.4 all-to-all-start.1
  252.8 27.4 %collective-permute-done.16 = bf16[256,2048]{1,0:T(8,128)(2,1)S(1)} collective-permute-done((bf16[256,2048]{1,0:T(8,128)(2,1)}, bf16[256,2048]{1,0:T(8,128)(2,1)S(1)}, u32[]{:S(2)}, u32[]{:S(2)}) %collective-permute-start.16) | collective-permute-done | bytes 1048608 | tf_op jit(solution)/shard_map/ppermute | solution.py:196
  281.2 2.2 convolution_convert_fusion
  283.4 4.4 all-to-all-start.4
  287.8 6.7 %fusion.6 = f32[576,1536]{1,0:T(8,128)S(1)} fusion(bf16[576,2048]{1,0:T(8,128)(2,1)} %bitcast.36, bf16[1,2048,1536]{2,1,0:T(8,128)(2,1)} %param.29), kind=kOutput, calls=%fused_computation.6 | convolution fusion | flops 3623878656 | bytes 12189696 | tf_op jit(solution)/shard_map/dot_general | solution.py:157
  294.5 3.5 fusion.16
  298.0 19.3 %all-to-all-done.4 = bf16[8,72,2048]{2,1,0:T(8,128)(2,1)} async-done(((bf16[8,72,2048]{2,1,0:T(8,128)(2,1)}), bf16[8,72,2048]{2,1,0:T(8,128)(2,1)}, u32[]{:S(2)}, u32[]{:S(2)}) %all-to-all-start.4) | async-done | bytes 2359328 | tf_op jit(solution)/shard_map/all_to_all | solution.py:198
  317.2 4.4 all-to-all-start.2
  321.7 27.4 %collective-permute-done.17 = bf16[256,2048]{1,0:T(8,128)(2,1)S(1)} collective-permute-done((bf16[256,2048]{1,0:T(8,128)(2,1)}, bf16[256,2048]{1,0:T(8,128)(2,1)S(1)}, u32[]{:S(2)}, u32[]{:S(2)}) %collective-permute-start.17) | collective-permute-done | bytes 1048608 | tf_op jit(solution)/shard_map/ppermute | solution.py:196
  349.1 2.2 convolution_convert_fusion.3
  351.3 4.5 all-to-all-start
  355.9 6.7 %fusion.4 = f32[576,1536]{1,0:T(8,128)S(1)} fusion(bf16[576,2048]{1,0:T(8,128)(2,1)} %bitcast.50, bf16[1,2048,1536]{2,1,0:T(8,128)(2,1)} %param.29), kind=kOutput, calls=%fused_computation.4 | convolution fusion | flops 3623878656 | bytes 12189696 | tf_op jit(solution)/shard_map/dot_general | solution.py:157
  362.6 3.4 fusion.19
  366.0 19.2 %all-to-all-done = bf16[8,72,2048]{2,1,0:T(8,128)(2,1)} async-done(((bf16[8,72,2048]{2,1,0:T(8,128)(2,1)}), bf16[8,72,2048]{2,1,0:T(8,128)(2,1)}, u32[]{:S(2)}, u32[]{:S(2)}) %all-to-all-start) | async-done | bytes 2359328 | tf_op jit(solution)/shard_map/all_to_all | solution.py:198
  385.3 4.7 all-to-all-start.5
  390.1 3.8 fusion.29
  393.9 6.6 %fusion.2 = f32[576,1536]{1,0:T(8,128)S(1)} fusion(bf16[576,2048]{1,0:T(8,128)(2,1)} %bitcast.54, bf16[1,2048,1536]{2,1,0:T(8,128)(2,1)} %param.29), kind=kOutput, calls=%fused_computation.2 | convolution fusion | flops 3623878656 | bytes 12189696 | tf_op jit(solution)/shard_map/dot_general | solution.py:157
  400.5 3.5 fusion.22
  404.0 15.2 %all-to-all-done.5 = bf16[8,72,2048]{2,1,0:T(8,128)(2,1)} async-done(((bf16[8,72,2048]{2,1,0:T(8,128)(2,1)}), bf16[8,72,2048]{2,1,0:T(8,128)(2,1)}, u32[]{:S(2)}, u32[]{:S(2)}) %all-to-all-start.5) | async-done | bytes 2359328 | tf_op jit(solution)/shard_map/all_to_all | solution.py:208
  419.3 4.4 all-to-all-start.6
  423.7 3.7 fusion.30
  427.4 6.6 %fusion = f32[576,1536]{1,0:T(8,128)S(1)} fusion(bf16[576,2048]{1,0:T(8,128)(2,1)} %bitcast.58, bf16[1,2048,1536]{2,1,0:T(8,128)(2,1)} %param.29), kind=kOutput, calls=%fused_computation | convolution fusion | flops 3623878656 | bytes 12189696 | tf_op jit(solution)/shard_map/dot_general | solution.py:157
  434.0 3.5 fusion.25
  437.5 15.6 %all-to-all-done.6 = bf16[8,72,2048]{2,1,0:T(8,128)(2,1)} async-done(((bf16[8,72,2048]{2,1,0:T(8,128)(2,1)}), bf16[8,72,2048]{2,1,0:T(8,128)(2,1)}, u32[]{:S(2)}, u32[]{:S(2)}) %all-to-all-start.6) | async-done | bytes 2359328 | tf_op jit(solution)/shard_map/all_to_all | solution.py:208
  453.2 4.4 all-to-all-start.7
  457.9 3.7 fusion.31
  463.3 20.7 %collective-permute-done.18 = bf16[256,2048]{1,0:T(8,128)(2,1)} collective-permute-done((bf16[256,2048]{1,0:T(8,128)(2,1)}, bf16[256,2048]{1,0:T(8,128)(2,1)}, u32[]{:S(2)}, u32[]{:S(2)}) %collective-permute-start.18) | collective-permute-done | bytes 1048608 | tf_op jit(solution)/shard_map/ppermute | solution.py:216
  484.0 64.6 %collective-permute-done.19 = bf16[256,2048]{1,0:T(8,128)(2,1)} collective-permute-done((bf16[256,2048]{1,0:T(8,128)(2,1)}, bf16[256,2048]{1,0:T(8,128)(2,1)}, u32[]{:S(2)}, u32[]{:S(2)}) %collective-permute-start.19) | collective-permute-done | bytes 1048608 | tf_op jit(solution)/shard_map/ppermute | solution.py:216
  548.6 5.2 fusion.35
  (139 shorter events, 37.6 us)
Async XLA Ops:
  6.5 287.9 %copy-start = (bf16[1,768,2048]{2,1,0:T(8,128)(2,1)S(1)}, bf16[1,768,2048]{2,1,0:T(8,128)(2,1)}, u32[]{:S(2)}) copy-start(bf16[1,768,2048]{2,1,0:T(8,128)(2,1)} %param.30) | copy-start | bytes 9437188
  6.5 138.2 %all-gather.2.cloned.1.call-start = ((), (), s32[]{:S(2)}) async-start(), calls=%async_computation.8 | async-start | bytes 17301504 | tf_op jit(solution)/shard_map/all_gather | solution.py:242
  10.6 39.6 %collective-permute-start.12 = (f32[16,256]{1,0:T(8,128)}, f32[16,256]{1,0:T(8,128)}, u32[]{:S(2)}, u32[]{:S(2)}) collective-permute-start(f32[16,256]{1,0:T(8,128)} %get-tuple-element.65), channel_id=1, source_target_pairs={{0,1},{1,2},{2,3},{3,0},{4,5},{5,6},{6,7},{7,4},{8,9},{9,10},{10,1... | collective-permute-start | bytes 49160 | tf_op jit(solution)/shard_map/ppermute | solution.py:171
  21.9 1.7 copy-start.6
  36.7 2.0 copy-start.3
  38.6 53.0 %copy-start.25 = (f32[64]{0:T(128)S(1)}, f32[64]{0:T(128)}, u32[]{:S(2)}) copy-start(f32[64]{0:T(128)} %param.23) | copy-start | bytes 772
  40.7 53.5 %collective-permute-start = (bf16[2,128,512]{2,1,0:T(8,128)(2,1)}, bf16[2,128,512]{2,1,0:T(8,128)(2,1)S(1)}, u32[]{:S(2)}, u32[]{:S(2)}) collective-permute-start(bf16[2,128,512]{2,1,0:T(8,128)(2,1)} %get-tuple-element.41), channel_id=1, source_target_pairs={{0,1},{4,5},{8,9},{12,13},{16,17},{20,21},{24,25},{28,29}} | collective-permute-start | bytes 786440 | tf_op jit(solution)/shard_map/ppermute | solution.py:133
  44.2 50.0 %collective-permute-start.3 = (bf16[2,128,512]{2,1,0:T(8,128)(2,1)}, bf16[2,128,512]{2,1,0:T(8,128)(2,1)}, u32[]{:S(2)}, u32[]{:S(2)}) collective-permute-start(bf16[2,128,512]{2,1,0:T(8,128)(2,1)} %get-tuple-element.44), channel_id=1, source_target_pairs={{0,1},{4,5},{8,9},{12,13},{16,17},{20,21},{24,25},{28,29}} | collective-permute-start | bytes 786440 | tf_op jit(solution)/shard_map/ppermute | solution.py:133
  46.2 48.0 %collective-permute-start.6 = (bf16[2,128,512]{2,1,0:T(8,128)(2,1)}, bf16[2,128,512]{2,1,0:T(8,128)(2,1)}, u32[]{:S(2)}, u32[]{:S(2)}) collective-permute-start(bf16[2,128,512]{2,1,0:T(8,128)(2,1)} %get-tuple-element.43), channel_id=1, source_target_pairs={{0,1},{4,5},{8,9},{12,13},{16,17},{20,21},{24,25},{28,29}} | collective-permute-start | bytes 786440 | tf_op jit(solution)/shard_map/ppermute | solution.py:133
  48.2 46.0 %collective-permute-start.9 = (bf16[2,128,512]{2,1,0:T(8,128)(2,1)}, bf16[2,128,512]{2,1,0:T(8,128)(2,1)}, u32[]{:S(2)}, u32[]{:S(2)}) collective-permute-start(bf16[2,128,512]{2,1,0:T(8,128)(2,1)} %get-tuple-element.42), channel_id=1, source_target_pairs={{0,1},{4,5},{8,9},{12,13},{16,17},{20,21},{24,25},{28,29}} | collective-permute-start | bytes 786440 | tf_op jit(solution)/shard_map/ppermute | solution.py:133
  50.2 37.6 %collective-permute-start.13 = (f32[16,256]{1,0:T(8,128)}, f32[16,256]{1,0:T(8,128)S(1)}, u32[]{:S(2)}, u32[]{:S(2)}) collective-permute-start(f32[16,256]{1,0:T(8,128)} %collective-permute-done.12), channel_id=1, source_target_pairs={{0,1},{1,2},{2,3},{3,0},{4,5},{5,6},{6,7},{7,4},{8,9},{9,10},{10,1... | collective-permute-start | bytes 49160 | tf_op jit(solution)/shard_map/ppermute | solution.py:171
  87.8 5.6 %collective-permute-start.14 = (f32[16,256]{1,0:T(8,128)S(1)}, f32[16,256]{1,0:T(8,128)}, u32[]{:S(2)}, u32[]{:S(2)}) collective-permute-start(f32[16,256]{1,0:T(8,128)S(1)} %collective-permute-done.13), channel_id=1, source_target_pairs={{0,1},{1,2},{2,3},{3,0},{4,5},{5,6},{6,7},{7,4},{8,9},{9,10},{10,1... | collective-permute-start | bytes 49160 | tf_op jit(solution)/shard_map/ppermute | solution.py:171
  90.3 7.8 %copy-start.19 = (f32[72]{0:T(128)}, f32[72]{0:T(128)S(1)}, u32[]{:S(2)}) copy-start(f32[72]{0:T(128)S(1)} %iota_convert_fusion) | copy-start | bytes 868
  91.8 7.0 %copy-start.23 = (s32[8]{0:T(128)S(1)}, s32[8]{0:T(128)}, u32[]{:S(2)}) copy-start(s32[8]{0:T(128)} %multiply_add_fusion) | copy-start | bytes 100
  92.5 6.5 %copy-start.2 = (bf16[8,128,512]{2,1,0:T(8,128)(2,1)S(1)}, bf16[8,128,512]{2,1,0:T(8,128)(2,1)}, u32[]{:S(2)}) copy-start(bf16[8,128,512]{2,1,0:T(8,128)(2,1)} %copy-done.1) | copy-start | bytes 3145732
  96.0 2.9 collective-permute-start.1
  96.7 2.2 collective-permute-start.10
  97.4 1.5 collective-permute-start.4
  98.1 0.9 collective-permute-start.7
  98.9 5.0 copy-start.21
  99.0 6.5 %copy-start.7 = (bf16[256,4096]{1,0:T(8,128)(2,1)S(1)}, bf16[256,4096]{1,0:T(8,128)(2,1)}, u32[]{:S(2)}) copy-start(bf16[256,4096]{1,0:T(8,128)(2,1)} %x_ref.3) | copy-start | bytes 6291460
  99.0 6.5 %copy-start.8 = (bf16[256,4096]{1,0:T(8,128)(2,1)S(1)}, bf16[256,4096]{1,0:T(8,128)(2,1)}, u32[]{:S(2)}) copy-start(bf16[256,4096]{1,0:T(8,128)(2,1)} %gate_ref.1) | copy-start | bytes 6291460
  99.0 6.5 %copy-start.12 = (bf16[256,2048]{1,0:T(8,128)(2,1)S(1)}, bf16[256,2048]{1,0:T(8,128)(2,1)}, u32[]{:S(2)}) copy-start(bf16[256,2048]{1,0:T(8,128)(2,1)} %bc_ref.3) | copy-start | bytes 3145732
  100.8 4.2 collective-permute-start.2
  101.6 3.5 collective-permute-start.5
  102.3 2.9 collective-permute-start.8
  103.0 2.3 collective-permute-start.11
  103.9 1.6 copy-start.13
  105.1 2.5 copy-start.4
  117.8 38.4 %copy-start.22 = (f32[2048]{0:T(1024)S(1)}, f32[2048]{0:T(1024)}, u32[]{:S(2)}) copy-start(f32[2048]{0:T(1024)} %param.26) | copy-start | bytes 24580
  155.9 3.3 copy-start.14
  156.5 2.7 copy-start.15
  159.2 89.1 %all-to-all-start.3 = ((bf16[8,72,2048]{2,1,0:T(8,128)(2,1)}), bf16[8,72,2048]{2,1,0:T(8,128)(2,1)}, u32[]{:S(2)}, u32[]{:S(2)}) async-start(bf16[8,72,2048]{2,1,0:T(8,128)(2,1)} %bitcast.164), calls=%async_computation.3 | async-start | bytes 4718592 | tf_op jit(solution)/shard_map/all_to_all | solution.py:198
  163.8 80.4 %collective-permute-start.15 = (bf16[256,2048]{1,0:T(8,128)(2,1)}, bf16[256,2048]{1,0:T(8,128)(2,1)S(1)}, u32[]{:S(2)}, u32[]{:S(2)}) collective-permute-start(bf16[256,2048]{1,0:T(8,128)(2,1)} %copy-done.15), channel_id=1, source_target_pairs={{0,1},{1,2},{2,3},{3,0},{4,5},{5,6},{6,7},{7,4},{8,9},{9,10},{10,1... | collective-permute-start | bytes 3145736 | tf_op jit(solution)/shard_map/ppermute | solution.py:196
  248.3 35.1 %all-to-all-start.1 = ((bf16[8,72,2048]{2,1,0:T(8,128)(2,1)}), bf16[8,72,2048]{2,1,0:T(8,128)(2,1)}, u32[]{:S(2)}, u32[]{:S(2)}) async-start(bf16[8,72,2048]{2,1,0:T(8,128)(2,1)} %bitcast.162), calls=%async_computation.1 | async-start | bytes 4718592 | tf_op jit(solution)/shard_map/all_to_all | solution.py:198
  252.7 27.5 %collective-permute-start.16 = (bf16[256,2048]{1,0:T(8,128)(2,1)}, bf16[256,2048]{1,0:T(8,128)(2,1)S(1)}, u32[]{:S(2)}, u32[]{:S(2)}) collective-permute-start(bf16[256,2048]{1,0:T(8,128)(2,1)} %copy-done.17), channel_id=1, source_target_pairs={{0,1},{1,2},{2,3},{3,0},{4,5},{5,6},{6,7},{7,4},{8,9},{9,10},{10,1... | collective-permute-start | bytes 3145736 | tf_op jit(solution)/shard_map/ppermute | solution.py:196
  283.4 33.9 %all-to-all-start.4 = ((bf16[8,72,2048]{2,1,0:T(8,128)(2,1)}), bf16[8,72,2048]{2,1,0:T(8,128)(2,1)}, u32[]{:S(2)}, u32[]{:S(2)}) async-start(bf16[8,72,2048]{2,1,0:T(8,128)(2,1)} %bitcast.165), calls=%async_computation.4 | async-start | bytes 4718592 | tf_op jit(solution)/shard_map/all_to_all | solution.py:198
  317.2 34.1 %all-to-all-start.2 = ((bf16[8,72,2048]{2,1,0:T(8,128)(2,1)}), bf16[8,72,2048]{2,1,0:T(8,128)(2,1)}, u32[]{:S(2)}, u32[]{:S(2)}) async-start(bf16[8,72,2048]{2,1,0:T(8,128)(2,1)} %bitcast.168), calls=%async_computation.2 | async-start | bytes 4718592 | tf_op jit(solution)/shard_map/all_to_all | solution.py:208
  321.7 27.5 %collective-permute-start.17 = (bf16[256,2048]{1,0:T(8,128)(2,1)}, bf16[256,2048]{1,0:T(8,128)(2,1)S(1)}, u32[]{:S(2)}, u32[]{:S(2)}) collective-permute-start(bf16[256,2048]{1,0:T(8,128)(2,1)} %copy-done.16), channel_id=1, source_target_pairs={{0,1},{1,2},{2,3},{3,0},{4,5},{5,6},{6,7},{7,4},{8,9},{9,10},{10,1... | collective-permute-start | bytes 3145736 | tf_op jit(solution)/shard_map/ppermute | solution.py:196
  351.3 4.5 copy-start.24
  351.3 34.0 %all-to-all-start = ((bf16[8,72,2048]{2,1,0:T(8,128)(2,1)}), bf16[8,72,2048]{2,1,0:T(8,128)(2,1)}, u32[]{:S(2)}, u32[]{:S(2)}) async-start(bf16[8,72,2048]{2,1,0:T(8,128)(2,1)} %bitcast.163), calls=%async_computation | async-start | bytes 4718592 | tf_op jit(solution)/shard_map/all_to_all | solution.py:198
  385.3 4.8 copy-start.20
  385.3 34.0 %all-to-all-start.5 = ((bf16[8,72,2048]{2,1,0:T(8,128)(2,1)}), bf16[8,72,2048]{2,1,0:T(8,128)(2,1)}, u32[]{:S(2)}, u32[]{:S(2)}) async-start(bf16[8,72,2048]{2,1,0:T(8,128)(2,1)} %bitcast.167), calls=%async_computation.5 | async-start | bytes 4718592 | tf_op jit(solution)/shard_map/all_to_all | solution.py:208
  419.3 33.9 %all-to-all-start.6 = ((bf16[8,72,2048]{2,1,0:T(8,128)(2,1)}), bf16[8,72,2048]{2,1,0:T(8,128)(2,1)}, u32[]{:S(2)}, u32[]{:S(2)}) async-start(bf16[8,72,2048]{2,1,0:T(8,128)(2,1)} %bitcast.169), calls=%async_computation.6 | async-start | bytes 4718592 | tf_op jit(solution)/shard_map/all_to_all | solution.py:208
  453.2 95.5 %all-to-all-start.7 = ((bf16[8,72,2048]{2,1,0:T(8,128)(2,1)}), bf16[8,72,2048]{2,1,0:T(8,128)(2,1)}, u32[]{:S(2)}, u32[]{:S(2)}) async-start(bf16[8,72,2048]{2,1,0:T(8,128)(2,1)} %bitcast.166), calls=%async_computation.7 | async-start | bytes 4718592 | tf_op jit(solution)/shard_map/all_to_all | solution.py:208
  457.5 26.5 %collective-permute-start.18 = (bf16[256,2048]{1,0:T(8,128)(2,1)}, bf16[256,2048]{1,0:T(8,128)(2,1)}, u32[]{:S(2)}, u32[]{:S(2)}) collective-permute-start(bf16[256,2048]{1,0:T(8,128)(2,1)} %fusion.29), channel_id=1, source_target_pairs={{0,3},{1,0},{2,1},{3,2},{4,7},{5,4},{6,5},{7,6},{8,11},{9,8},{10,9... | collective-permute-start | bytes 3145736 | tf_op jit(solution)/shard_map/ppermute | solution.py:216
  457.9 90.7 %collective-permute-start.19 = (bf16[256,2048]{1,0:T(8,128)(2,1)}, bf16[256,2048]{1,0:T(8,128)(2,1)}, u32[]{:S(2)}, u32[]{:S(2)}) collective-permute-start(bf16[256,2048]{1,0:T(8,128)(2,1)} %fusion.30), channel_id=1, source_target_pairs={{0,2},{1,3},{2,0},{3,1},{4,6},{5,7},{6,4},{7,5},{8,10},{9,11},{10,... | collective-permute-start | bytes 3145736 | tf_op jit(solution)/shard_map/ppermute | solution.py:216
  461.6 87.0 %collective-permute-start.20 = (bf16[256,2048]{1,0:T(8,128)(2,1)}, bf16[256,2048]{1,0:T(8,128)(2,1)}, u32[]{:S(2)}, u32[]{:S(2)}) collective-permute-start(bf16[256,2048]{1,0:T(8,128)(2,1)} %fusion.31), channel_id=1, source_target_pairs={{0,1},{1,2},{2,3},{3,0},{4,5},{5,6},{6,7},{7,4},{8,9},{9,10},{10,1... | collective-permute-start | bytes 3145736 | tf_op jit(solution)/shard_map/ppermute | solution.py:216
  (8 other events, 9.1 us)
Sparse Core Ops, SparseCore 0:
  10.2 134.5 all-gather.1

commit v3 on v2

--- a/solution.py
+++ b/solution.py
@@ -153,10 +153,23 @@
     )
 
 
-def experts_of(arrived, gate_up, down_proj):
+def swap(rows):
+    dp_size = lax.axis_size("dp")
+    blocks = rows.reshape(dp_size, -1, rows.shape[-1])
+    return lax.all_to_all(blocks, "dp", split_axis=0, concat_axis=0, tiled=True).reshape(rows.shape)
+
+
+def active_of(arrived, gate_up):
     hidden = jnp.dot(arrived, gate_up, preferred_element_type=f32)
-    active = (jax.nn.silu(hidden[:, :FF]) * hidden[:, FF:]).astype(bf16)
-    return jnp.dot(active, down_proj, preferred_element_type=f32).astype(bf16)
+    return (jax.nn.silu(hidden[:, :FF]) * hidden[:, FF:]).astype(bf16)
+
+
+def taken_by(place, slots):
+    return (jnp.transpose(place)[:, None, :] == slots[None, :, None]).astype(bf16).reshape(-1, place.shape[0])
+
+
+def spread_by(place, gains, slots):
+    return jnp.where(place[:, :, None] == slots, gains[:, :, None], 0.0).astype(bf16).reshape(place.shape[0], -1)
 
 
 def routed(normed, expert_ids, route_weights, gate_up, down_proj):
@@ -169,7 +182,7 @@
     routes = [jnp.concatenate([expert_ids.T.astype(f32), route_weights.T], axis=0)]
     for _ in range(seq_size - 1):
         routes.append(lax.ppermute(routes[-1], "seq", ring))
-    routes = jnp.stack(routes)
+    routes = jnp.roll(jnp.stack(routes[::-1]), rank + 1, axis=0)
     all_ids = jnp.transpose(routes[:, :TOP], (0, 2, 1)).astype(jnp.int32)
     all_weights = jnp.transpose(routes[:, TOP:], (0, 2, 1))
     here = jnp.arange(dp_size, dtype=jnp.int32) * seq_size + rank
@@ -180,42 +193,33 @@
     earlier = (ids[:, None] > ids[None, :]).astype(bf16)
     place = jnp.einsum("ij,sjd->sid", earlier, chosen.astype(bf16), preferred_element_type=f32)
     place = jnp.where(chosen, place, -1.0)
-    slots = jnp.arange(capacity, dtype=jnp.int32).astype(f32)
-    current = normed
-    arrivals, spreads = [], []
-    for offset in range(seq_size):
-        place_here = place[offset]
-        gains_here = gains[offset]
-        taken = jnp.transpose(place_here)[:, None, :] == slots[None, :, None]
-        outgoing = jnp.dot(
-            taken.astype(bf16).reshape(dp_size * capacity, rows), current, preferred_element_type=f32
-        ).astype(bf16)
-        spread = jnp.where(place_here[:, :, None] == slots, gains_here[:, :, None], 0.0)
-        spreads.append(spread.astype(bf16).reshape(rows, dp_size * capacity))
-        if offset < seq_size - 1:
-            current = lax.ppermute(current, "seq", ring)
-        arrivals.append(
-            lax.all_to_all(outgoing.reshape(dp_size, capacity, D), "dp", split_axis=0, concat_axis=0, tiled=True)
-        )
-    order = list(range(1, seq_size)) + [0]
-    parts = []
-    total = None
-    for turn, offset in enumerate(order):
-        arrived = arrivals[offset]
-        if turn >= 2:
-            arrived, parts[turn - 2] = lax.optimization_barrier((arrived, parts[turn - 2]))
-        result = experts_of(arrived.reshape(-1, D), gate_up[0], down_proj[0])
-        returned = lax.all_to_all(
-            result.reshape(dp_size, capacity, D), "dp", split_axis=0, concat_axis=0, tiled=True
-        )
-        part = jnp.dot(spreads[offset], returned.reshape(-1, D), preferred_element_type=f32)
-        parts.append(part.astype(bf16) if offset else part)
-    for turn, offset in enumerate(order):
-        part = parts[turn]
-        if offset:
-            part = lax.ppermute(part, "seq", [(i, (i - offset) % seq_size) for i in range(seq_size)]).astype(f32)
-        total = part if total is None else total + part
-    return total
+    own_place = lax.dynamic_index_in_dim(place, rank, 0, keepdims=False)
+    own_gains = lax.dynamic_index_in_dim(gains, rank, 0, keepdims=False)
+    ahead = lax.rem(rank - jnp.arange(seq_size) + seq_size, seq_size) - 1
+    base = (ahead * capacity).astype(f32)[:, None, None]
+    place = jnp.where(chosen & (ahead >= 0)[:, None, None], place + base, -1.0).reshape(-1, dp_size)
+    gains = gains.reshape(-1, dp_size)
+    own_slots = jnp.arange(capacity, dtype=jnp.int32).astype(f32)
+    slots = jnp.arange((seq_size - 1) * capacity, dtype=jnp.int32).astype(f32)
+
+    tokens = lax.all_gather(normed, "seq", tiled=True)
+    own_out = jnp.dot(taken_by(own_place, own_slots), normed, preferred_element_type=f32).astype(bf16)
+    own_active = active_of(swap(own_out), gate_up[0])
+    own_result = jnp.dot(own_active, down_proj[0], preferred_element_type=f32).astype(bf16)
+    own_back = swap(own_result)
+    tokens, own_back = lax.optimization_barrier((tokens, own_back))
+
+    outgoing = jnp.dot(taken_by(place, slots), tokens, preferred_element_type=f32).astype(bf16)
+    active = active_of(swap(outgoing), gate_up[0])
+    spread = spread_by(place, gains, slots)
+    sums = []
+    half = D // 2
+    for at in (slice(0, half), slice(half, D)):
+        result = jnp.dot(active, down_proj[0][:, at], preferred_element_type=f32).astype(bf16)
+        part = jnp.dot(spread, swap(result), preferred_element_type=f32).astype(bf16)
+        sums.append(lax.psum_scatter(part, "seq", scatter_dimension=0, tiled=True))
+    own = jnp.dot(spread_by(own_place, own_gains, own_slots), own_back, preferred_element_type=f32)
+    return own + jnp.concatenate(sums, axis=1).astype(f32)
 
 
 def body(

time: 562 us -> 554 us (0.986)
  blocking collectives: 0 us -> 160 us
  waiting for transfers between devices: 320 us -> 240 us
  starting transfers between devices: 93.6 us -> 26.1 us
  matrix products: 79.1 us -> 68.9 us
  local copies, waits for them, and re-layouts: 19.8 us -> 10.5 us
    ppermute x6 -> x0, waiting for transfers between devices: 185 us -> none  [the longest x3 100 us: routed(): current = lax.ppermute(current, 'seq', ring)]
    all_to_all x0 -> x3, blocking collectives: none -> 160 us  [swap(): lax.all_to_all(blocks, 'dp', split_axis=0, concat_axis=0, tiled=True)]
    all_gather x0 -> x1, waiting for transfers between devices: none -> 51.6 us  [routed(): tokens = lax.all_gather(normed, 'seq', tiled=True)]
    reduce_scatter x0 -> x2, waiting for transfers between devices: none -> 39.8 us  [routed(): sums.append(lax.psum_scatter(part, 'seq', scatter_dimension=0, tiled=True))]
    ppermute x6 -> x0, starting transfers between devices: 37.3 us -> none  [the longest x3 35.2 us: routed(): current = lax.ppermute(current, 'seq', ring)]
    all_to_all x8 -> x2, starting transfers between devices: 35.7 us -> 8.1 us  [swap(): lax.all_to_all(blocks, 'dp', split_axis=0, concat_axis=0, tiled=True)]
    ppermute x3, waiting for transfers between devices: 38 us -> 46.1 us  [routed(): routes.append(lax.ppermute(routes[-1], 'seq', ring))]
    unnamed x52 -> x46, local copies, waits for them, and re-layouts: 13 us -> 5.21 us
  transfers between devices with their start and end apart: 30 -> 21, of which waited for: 12 -> 8; matrix products, arithmetic and copies ran while one was open for 14% -> 6% of each run, Pallas kernels for 3% -> 4%
where the time goes in v3:
time: 554 us; the launch traced here: 553 us
  waiting for transfers between devices  240 us (43%)
  blocking collectives  160 us (29%)
  matrix products  68.9 us (12%)
  starting transfers between devices  26.1 us (5%)
  Pallas kernels  19.5 us (4%)
  between operations  15.1 us (3%)
  other arithmetic  12.6 us (2%)
  local copies, waits for them, and re-layouts  10.5 us (2%)
    all_to_all x3, blocking collectives, swap(): lax.all_to_all(blocks, 'dp', split_axis=0, concat_axis=0, tiled=True)  160 us
    all_to_all x2, waiting for transfers between devices, swap(): lax.all_to_all(blocks, 'dp', split_axis=0, concat_axis=0, tiled=True)  68.9 us
    all_gather x1, waiting for transfers between devices, routed(): tokens = lax.all_gather(normed, 'seq', tiled=True)  51.6 us
    ppermute x3, waiting for transfers between devices, routed(): routes.append(lax.ppermute(routes[-1], 'seq', ring))  46.1 us
    reduce_scatter x2, waiting for transfers between devices, routed(): sums.append(lax.psum_scatter(part, 'seq', scatter_dimension=0, tiled=True))  39.8 us
    all_gather x1, waiting for transfers between devices, body(): weight = lax.all_gather(own, ('seq', 'dp'), tiled=True)  34 us
    dot_general x2, matrix products, active_of(): hidden = jnp.dot(arrived, gate_up, preferred_element_type=f32)  17.5 us
    ppermute x12, starting transfers between devices, mixer(): total = total + lax.ppermute(sent, 'seq', [(hop, hop + 1)])  14.7 us
  transfers between devices with their start and end apart: 21, of which 8 were waited for; matrix products, arithmetic and copies ran while one was open for 6% of the time, Pallas kernels for 4%

profile of v3, /device:TPU:0, one launch (start us, length us, event | category | flops | bytes accessed | tf_op | source)
XLA Modules:
  0.0 553.0 jit_solution(3756779944369571878)
XLA Ops:
  6.5 2.0 constant_dynamic-slice_fusion
  8.7 0.8 reduce-window.8
  12.0 1.1 fusion.40
  13.3 0.9 multiply_bitcast_fusion
  14.2 1.3 copy.34.cols_ref
  16.8 1.2 copy-done.5
  18.1 1.2 copy-done.6
  19.3 10.5 %shard_map.154 = (f32[256,4096]{1,0:T(8,128)S(1)}, bf16[8,128,512]{2,1,0:T(8,128)(2,1)S(1)}) custom-call(bf16[256,4096]{1,0:T(8,128)(2,1)S(1)} %copy-done.2, bf16[256,2048]{1,0:T(8,128)(2,1)S(1)} %copy-done.6, f32[8,256,24]{2,1,0:T(8,128)S(1)} %copy-done.5, f32[8,8,256]{2,1,0:T(8,128)S(1)} %bitcast.116, s32[256,1]{1,0:T(8,128)S(1)} %copy.35.seg_col_ref, ...), custom_call_target="tpu_custom_call" | custom-call | flops 10000000000 | bytes 10000000 | tf_op jit(solution)/shard_map/pallas_call | solution.py:105
  29.8 1.9 copy-done
  31.8 1.1 fusion.27
  32.8 4.9 collective-permute-start
  37.8 1.3 collective-permute-start.3
  39.1 1.3 collective-permute-start.6
  40.4 1.3 collective-permute-start.9
  41.9 38.7 %collective-permute-done.12 = f32[16,256]{1,0:T(8,128)S(1)} collective-permute-done((f32[16,256]{1,0:T(8,128)S(1)}, f32[16,256]{1,0:T(8,128)S(1)}, u32[]{:S(2)}, u32[]{:S(2)}) %collective-permute-start.12) | collective-permute-done | bytes 16416 | tf_op jit(solution)/shard_map/ppermute | solution.py:184
  80.6 2.5 collective-permute-start.13
  83.1 3.1 collective-permute-done.13
  87.4 4.3 collective-permute-done.14
  92.1 0.7 collective-permute-start.1
  95.5 0.8 collective-permute-start.2
  96.3 0.8 collective-permute-start.5
  97.2 0.8 collective-permute-start.8
  99.3 8.9 %shard_map.155 = bf16[256,4096]{1,0:T(8,128)(2,1)S(1)} custom-call(f32[256,4096]{1,0:T(8,128)S(1)} %copy-done.1, bf16[256,4096]{1,0:T(8,128)(2,1)S(1)} %copy-done.3, bf16[256,2048]{1,0:T(8,128)(2,1)S(1)} %copy-done.7, bf16[256,4096]{1,0:T(8,128)(2,1)S(1)} %copy-done.4, bf16[8,128,512]{2,1,0:T(8,128)(2,1)S(1)} %pad_maximum_fusion.state_ref, ...), custom_call_target="tpu_custom_call" | custom-call | flops 1000000000 | bytes 10000000 | tf_op jit(solution)/shard_map/pallas_call | solution.py:136
  108.3 34.0 %all-gather.3.cloned.1.call-done = bf16[4096,2048]{1,0:T(8,128)(2,1)} async-done(((bf16[128,2048]{1,0:T(8,128)(2,1)}), bf16[4096,2048]{1,0:T(8,128)(2,1)}) %all-gather.3.cloned.1.call-update) | async-done | bytes 16777232 | tf_op jit(solution)/shard_map/all_gather | solution.py:246
  142.3 8.6 %fusion.15 = bf16[256,2048]{1,0:T(8,128)(2,1)S(1)} fusion(bf16[256,4096]{1,0:T(8,128)(2,1)S(1)} %shard_map.155, bf16[4096,2048]{1,0:T(8,128)(2,1)} %all-gather.3.cloned.1.call-done, bf16[256,2048]{1,0:T(8,128)(2,1)} %param.16), kind=kOutput, calls=%fused_computation.30 | convolution fusion | flops 4296540160 | bytes 20971520 | tf_op jit(solution)/shard_map/dot_general | solution.py:250
  151.9 1.3 fusion.19
  153.5 2.2 convolution_convert_fusion.4
  155.8 32.0 %all_to_all.25 = bf16[8,72,2048]{2,1,0:T(8,128)(2,1)S(1)} all-to-all(bf16[8,72,2048]{2,1,0:T(8,128)(2,1)S(1)} %bitcast.120), channel_id=1, replica_groups=mesh['dp'=8,'seq'=4] {'dp'}, dimensions={0} | all-to-all | bytes 4718592 | tf_op jit(solution)/shard_map/all_to_all | solution.py:159
  187.7 3.8 fusion.2
  191.6 3.5 convolution_convert_fusion.3
  195.1 3.6 all-to-all-start.1
  198.8 2.3 bitcast_compare_fusion
  201.2 26.9 %all-to-all-done.1 = bf16[8,72,2048]{2,1,0:T(8,128)(2,1)S(1)} async-done(((bf16[8,72,2048]{2,1,0:T(8,128)(2,1)}), bf16[8,72,2048]{2,1,0:T(8,128)(2,1)S(1)}, u32[]{:S(2)}, u32[]{:S(2)}) %all-to-all-start.1) | async-done | bytes 2359328 | tf_op jit(solution)/shard_map/all_to_all | solution.py:159
  228.1 51.6 %all-gather.5.cloned.1.call-done = bf16[1024,2048]{1,0:T(8,128)(2,1)} async-done(((bf16[256,2048]{1,0:T(8,128)(2,1)}), bf16[1024,2048]{1,0:T(8,128)(2,1)}) %all-gather.5.cloned.1.call-update) | async-done | bytes 4194320 | tf_op jit(solution)/shard_map/all_gather | solution.py:205
  279.7 10.1 %convolution_convert_fusion = bf16[1728,2048]{1,0:T(8,128)(2,1)S(1)} fusion(pred[1728,1024]{1,0:T(32,128)(4,1)} %bitcast_compare_fusion, bf16[1024,2048]{1,0:T(8,128)(2,1)} %all-gather.5.cloned.1.call-done), kind=kOutput, calls=%fused_computation | convolution fusion | flops 7251296256 | bytes 13041664 | tf_op jit(solution)/shard_map/dot_general | solution.py:212
  289.9 83.5 %all_to_all.26 = bf16[8,216,2048]{2,1,0:T(8,128)(2,1)S(1)} all-to-all(bf16[8,216,2048]{2,1,0:T(8,128)(2,1)S(1)} %bitcast.122), channel_id=1, replica_groups=mesh['dp'=8,'seq'=4] {'dp'}, dimensions={0} | all-to-all | bytes 14155776 | tf_op jit(solution)/shard_map/all_to_all | solution.py:159
  373.3 13.7 %fusion = f32[1728,1536]{1,0:T(8,128)S(1)} fusion(bf16[1728,2048]{1,0:T(8,128)(2,1)S(1)} %bitcast.123, bf16[1,2048,1536]{2,1,0:T(8,128)(2,1)} %param.29), kind=kOutput, calls=%fused_computation.3 | convolution fusion | flops 10871635968 | bytes 23986176 | tf_op jit(solution)/shard_map/dot_general | solution.py:163
  387.0 1.8 fusion.4
  388.9 4.4 convolution_convert_fusion.2
  393.3 4.5 all-to-all-start.3
  398.0 42.0 %all-to-all-done.3 = bf16[8,216,1024]{2,1,0:T(8,128)(2,1)} async-done(((bf16[8,216,1024]{2,1,0:T(8,128)(2,1)}), bf16[8,216,1024]{2,1,0:T(8,128)(2,1)}, u32[]{:S(2)}, u32[]{:S(2)}) %all-to-all-start.3) | async-done | bytes 3538976 | tf_op jit(solution)/shard_map/all_to_all | solution.py:159
  439.9 7.4 %bitcast_convert_fusion.1 = bf16[1024,1024]{1,0:T(8,128)(2,1)} fusion(bf16[8,216,1024]{2,1,0:T(8,128)(2,1)} %all-to-all-done.3, bf16[1024,8]{0,1:T(8,128)(2,1)S(1)} %bitcast.134, f32[1024,8]{0,1:T(8,128)S(1)} %bitcast.132, f32[216]{0:T(256)S(1)} %iota_convert_fusion), kind=kOutput, calls=%fused_computation.12 | convolution fusion | flops 3628466176 | bytes 5686112 | tf_op jit(solution)/shard_map/dot_general | solution.py:219
  447.4 5.1 convolution_convert_fusion.1
  452.5 44.5 %all_to_all.27 = bf16[8,216,1024]{2,1,0:T(8,128)(2,1)S(1)} all-to-all(bf16[8,216,1024]{2,1,0:T(8,128)(2,1)S(1)} %bitcast.125), channel_id=1, replica_groups=mesh['dp'=8,'seq'=4] {'dp'}, dimensions={0} | all-to-all | bytes 7077888 | tf_op jit(solution)/shard_map/all_to_all | solution.py:159
  497.0 5.4 bitcast_convert_fusion
  502.5 0.9 fusion.26
  503.3 39.8 %reduce-scatter.5.cloned.1.call-done = bf16[256,1024]{1,0:T(8,128)(2,1)} async-done(((bf16[1024,1024]{1,0:T(8,128)(2,1)}), bf16[256,1024]{1,0:T(8,128)(2,1)}) %reduce-scatter.5.cloned.1.call-update) | async-done | bytes 524304 | tf_op jit(solution)/shard_map/reduce_scatter | solution.py:220
  543.1 3.3 fusion.16
  (125 shorter events, 10.1 us)
Async XLA Ops:
  6.5 10.3 %copy-start.2 = (bf16[256,4096]{1,0:T(8,128)(2,1)S(1)}, bf16[256,4096]{1,0:T(8,128)(2,1)}, u32[]{:S(2)}) copy-start(bf16[256,4096]{1,0:T(8,128)(2,1)} %x_ref.3) | copy-start | bytes 6291460
  6.5 135.7 %all-gather.3.cloned.1.call-start = ((), (), s32[]{:S(2)}) async-start(), calls=%async_computation.7 | async-start | bytes 17301504 | tf_op jit(solution)/shard_map/all_gather | solution.py:246
  8.6 271.1 %all-gather.5.cloned.1.call-start = ((), (), s32[]{:S(2)}) async-start(), calls=%async_computation.8 | async-start | bytes 5242880 | tf_op jit(solution)/shard_map/all_gather | solution.py:205
  16.8 1.2 copy-start.5
  18.1 1.2 copy-start.6
  19.3 22.5 %copy-start.14 = (s32[256,8]{0,1:T(8,128)S(1)}, s32[256,8]{0,1:T(8,128)}, u32[]{:S(2)}) copy-start(s32[256,8]{0,1:T(8,128)} %param.27) | copy-start | bytes 24580
  19.3 22.5 %copy-start.12 = (f32[256,8]{0,1:T(8,128)S(1)}, f32[256,8]{0,1:T(8,128)}, u32[]{:S(2)}) copy-start(f32[256,8]{0,1:T(8,128)} %param.28) | copy-start | bytes 24580
  29.8 1.9 copy-start
  31.8 55.4 %copy-start.15 = (f32[64]{0:T(128)S(1)}, f32[64]{0:T(128)}, u32[]{:S(2)}) copy-start(f32[64]{0:T(128)} %param.23) | copy-start | bytes 772
  32.8 58.9 %collective-permute-start = (bf16[2,128,512]{2,1,0:T(8,128)(2,1)}, bf16[2,128,512]{2,1,0:T(8,128)(2,1)S(1)}, u32[]{:S(2)}, u32[]{:S(2)}) collective-permute-start(bf16[2,128,512]{2,1,0:T(8,128)(2,1)} %get-tuple-element.37), channel_id=1, source_target_pairs={{0,1},{4,5},{8,9},{12,13},{16,17},{20,21},{24,25},{28,29}} | collective-permute-start | bytes 786440 | tf_op jit(solution)/shard_map/ppermute | solution.py:133
  37.8 53.9 %collective-permute-start.3 = (bf16[2,128,512]{2,1,0:T(8,128)(2,1)}, bf16[2,128,512]{2,1,0:T(8,128)(2,1)S(1)}, u32[]{:S(2)}, u32[]{:S(2)}) collective-permute-start(bf16[2,128,512]{2,1,0:T(8,128)(2,1)} %get-tuple-element.40), channel_id=1, source_target_pairs={{0,1},{4,5},{8,9},{12,13},{16,17},{20,21},{24,25},{28,29}} | collective-permute-start | bytes 786440 | tf_op jit(solution)/shard_map/ppermute | solution.py:133
  39.1 52.6 %collective-permute-start.6 = (bf16[2,128,512]{2,1,0:T(8,128)(2,1)}, bf16[2,128,512]{2,1,0:T(8,128)(2,1)S(1)}, u32[]{:S(2)}, u32[]{:S(2)}) collective-permute-start(bf16[2,128,512]{2,1,0:T(8,128)(2,1)} %get-tuple-element.39), channel_id=1, source_target_pairs={{0,1},{4,5},{8,9},{12,13},{16,17},{20,21},{24,25},{28,29}} | collective-permute-start | bytes 786440 | tf_op jit(solution)/shard_map/ppermute | solution.py:133
  40.4 51.3 %collective-permute-start.9 = (bf16[2,128,512]{2,1,0:T(8,128)(2,1)}, bf16[2,128,512]{2,1,0:T(8,128)(2,1)S(1)}, u32[]{:S(2)}, u32[]{:S(2)}) collective-permute-start(bf16[2,128,512]{2,1,0:T(8,128)(2,1)} %get-tuple-element.38), channel_id=1, source_target_pairs={{0,1},{4,5},{8,9},{12,13},{16,17},{20,21},{24,25},{28,29}} | collective-permute-start | bytes 786440 | tf_op jit(solution)/shard_map/ppermute | solution.py:133
  41.8 38.8 %collective-permute-start.12 = (f32[16,256]{1,0:T(8,128)S(1)}, f32[16,256]{1,0:T(8,128)S(1)}, u32[]{:S(2)}, u32[]{:S(2)}) collective-permute-start(f32[16,256]{1,0:T(8,128)S(1)} %pad_maximum_fusion.1), channel_id=1, source_target_pairs={{0,1},{1,2},{2,3},{3,0},{4,5},{5,6},{6,7},{7,4},{8,9},{9,10},{10,1... | collective-permute-start | bytes 49160 | tf_op jit(solution)/shard_map/ppermute | solution.py:184
  80.6 5.6 %collective-permute-start.13 = (f32[16,256]{1,0:T(8,128)S(1)}, f32[16,256]{1,0:T(8,128)S(1)}, u32[]{:S(2)}, u32[]{:S(2)}) collective-permute-start(f32[16,256]{1,0:T(8,128)S(1)} %collective-permute-done.12), channel_id=1, source_target_pairs={{0,1},{1,2},{2,3},{3,0},{4,5},{5,6},{6,7},{7,4},{8,9},{9,10},{10,1... | collective-permute-start | bytes 49160 | tf_op jit(solution)/shard_map/ppermute | solution.py:184
  86.1 5.5 %collective-permute-start.14 = (f32[16,256]{1,0:T(8,128)S(1)}, f32[16,256]{1,0:T(8,128)S(1)}, u32[]{:S(2)}, u32[]{:S(2)}) collective-permute-start(f32[16,256]{1,0:T(8,128)S(1)} %collective-permute-done.13), channel_id=1, source_target_pairs={{0,1},{1,2},{2,3},{3,0},{4,5},{5,6},{6,7},{7,4},{8,9},{9,10},{10,1... | collective-permute-start | bytes 49160 | tf_op jit(solution)/shard_map/ppermute | solution.py:184
  92.1 2.8 collective-permute-start.1
  92.8 2.1 collective-permute-start.10
  93.5 1.4 collective-permute-start.4
  94.2 0.7 collective-permute-start.7
  94.9 4.4 copy-start.3
  94.9 4.4 copy-start.4
  95.5 3.8 copy-start.1
  95.5 3.8 copy-start.7
  95.5 3.8 copy-start.8
  95.5 3.3 collective-permute-start.2
  96.3 2.5 collective-permute-start.5
  97.2 1.8 collective-permute-start.8
  98.0 1.1 collective-permute-start.11
  108.3 43.6 %copy-start.13 = (f32[2048]{0:T(1024)S(1)}, f32[2048]{0:T(1024)}, u32[]{:S(2)}) copy-start(f32[2048]{0:T(1024)} %param.26) | copy-start | bytes 24580
  150.9 1.0 copy-start.9
  153.2 34.6 %slice-start = ((s8[6291456]{0:T(1024)(128)(4,1)}), s8[2097152]{0:T(1024)(128)(4,1)S(1)}, s32[]{:S(2)}) async-start(s8[6291456]{0:T(1024)(128)(4,1)} %bitcast.137), calls=%async_computation.11 | async-start | bytes 4194304
  153.5 34.2 %slice-start.1 = ((s8[6291456]{0:T(1024)(128)(4,1)}), s8[4194304]{0:T(1024)(128)(4,1)S(1)}, s32[]{:S(2)}) async-start(s8[6291456]{0:T(1024)(128)(4,1)} %bitcast.137), calls=%async_computation.12 | async-start | bytes 8388608
  187.7 3.8 copy-start.16
  195.1 33.0 %all-to-all-start.1 = ((bf16[8,72,2048]{2,1,0:T(8,128)(2,1)}), bf16[8,72,2048]{2,1,0:T(8,128)(2,1)S(1)}, u32[]{:S(2)}, u32[]{:S(2)}) async-start(bf16[8,72,2048]{2,1,0:T(8,128)(2,1)} %bitcast.126), calls=%async_computation.1 | async-start | bytes 4718592 | tf_op jit(solution)/shard_map/all_to_all | solution.py:159
  387.0 1.9 copy-start.17
  388.8 4.5 copy-start.11
  393.3 46.6 %all-to-all-start.3 = ((bf16[8,216,1024]{2,1,0:T(8,128)(2,1)}), bf16[8,216,1024]{2,1,0:T(8,128)(2,1)}, u32[]{:S(2)}, u32[]{:S(2)}) async-start(bf16[8,216,1024]{2,1,0:T(8,128)(2,1)} %bitcast.124), calls=%async_computation.3 | async-start | bytes 7077888 | tf_op jit(solution)/shard_map/all_to_all | solution.py:159
  397.8 105.5 %reduce-scatter.3.cloned.1.call-start = ((), (), s32[]{:S(2)}) async-start(), calls=%async_computation.9 | async-start | bytes 2621440 | tf_op jit(solution)/shard_map/reduce_scatter | solution.py:220
  447.3 95.8 %reduce-scatter.5.cloned.1.call-start = ((), (), s32[]{:S(2)}) async-start(), calls=%async_computation.10 | async-start | bytes 2621440 | tf_op jit(solution)/shard_map/reduce_scatter | solution.py:220
  497.0 46.1 %copy-start.10 = (bf16[256,2048]{1,0:T(8,128)(2,1)S(1)}, bf16[256,2048]{1,0:T(8,128)(2,1)}, u32[]{:S(2)}) copy-start(bf16[256,2048]{1,0:T(8,128)(2,1)} %copy-done.9) | copy-start | bytes 3145732
Sparse Core Ops, SparseCore 0:
  10.2 132.0 all-gather.2
  153.3 126.3 all-gather.4
  447.5 40.5 reduce-scatter.2
  502.6 40.5 reduce-scatter.4
